TPU v7x, 256 devices: a whole 4x4x8 slice. The times are simulated.
256 devices in a mesh: tm: 8 (over y_hi, x), space: 32 (over z, y_lo, core).
Axes of the slice: x: 4, y: 4 (y_hi: 2, y_lo: 2; y = y_hi * 2 + y_lo), z: 8, core: 2. Of those that a mesh axis runs over, the one named last changes fastest.
Arguments:
- initial: float32 [32, 131072], P(None, 'space'), may hold values from -6 to 6
- c_guess: float32 [8, 32, 131072], P('tm', None, 'space'), may hold values from -6 to 6
- forcing: float32 [64, 32, 131072], P('tm', None, 'space'), may hold values from -2 to 2
- fine_blocks: float32 [4, 16, 16], replicated, may hold values from -0.08 to 1.08, as said below
- coarse_blocks: float32 [4, 16, 16], replicated, may hold values from -0.08 to 1.08, as said below
Outputs:
- trajectory: float32 [64, 32, 131072], P('tm', None, 'space')
Inputs may be any that keep to these rules, and one draw needn't show every extreme that they name: `fine_blocks`: each of the four matrices is a diagonal (decays below 1, or couplings of 0.8) plus small independent entries. `coarse_blocks`: as fine_blocks, with stronger decays.
All inputs are finite; a program needn't handle non-finite values.
Results may differ from a plain program's by a relative error of at most 0.0001.
Values sent between devices are 32-bit elements; how exact they have to be, the bound alone decides.
No kernel may reach another device: no remote copies, remote signals or barrier semaphores. Data moves between devices by JAX's collectives and lax.ppermute only.
A program may use at most 64 MiB of HBM per device.

v0:
```python
import jax
import jax.numpy as jnp
from jax import lax
from jax.experimental import pallas as pl
from jax.experimental.pallas import tpu as pltpu
from jax.sharding import PartitionSpec as P

LANES = 128
REACH = 32
COND = 16
ROWS = 2 * COND
VMEM_LIMIT = 48 * 1024 * 1024


def iota(shape, axis):
    return lax.broadcasted_iota(jnp.int32, shape, axis)


def pack_edge(tile, base):
    lane = iota((8, LANES), 1)
    out = jnp.zeros((8, LANES), jnp.float32)
    for g in range(4):
        part = pltpu.roll(tile[8 * g : 8 * g + 8], (REACH * g - base) % LANES, 1)
        out = jnp.where(lane // REACH == g, part, out)
    return out


def unpack_edge(packed, base):
    return jnp.concatenate(
        [pltpu.roll(packed, (base - REACH * g) % LANES, 1) for g in range(4)], axis=0
    )


def halo_of_edges(from_left, from_right):
    lane = iota((ROWS, LANES), 1)
    right = jnp.where(lane < REACH, unpack_edge(from_right, 0), 0.0)
    return jnp.where(lane >= LANES - REACH, unpack_edge(from_left, LANES - REACH), right)


def pack_halo(halo):
    lane = iota((COND, LANES), 1)
    outer = (lane < REACH) | (lane >= LANES - REACH)
    return jnp.where(outer, halo[:COND], pltpu.roll(halo[COND:], LANES // 2, 1))


def unpack_halo(packed):
    return jnp.concatenate([packed, pltpu.roll(packed, LANES // 2, 1)], axis=0)


def join_halo(right, left):
    return jnp.where(iota((ROWS, LANES), 1) < LANES // 2, right, left)


def end_flags(index, size):
    at_left = jnp.where(index == 0, 1.0, 0.0).astype(jnp.float32)
    at_right = jnp.where(index == size - 1, 1.0, 0.0).astype(jnp.float32)
    return at_left, at_right


def fix_ends(last, halo, flags):
    at_left, at_right = flags
    lane = iota((ROWS, LANES), 1)
    row = iota((ROWS, LANES), 0)
    keep = 1.0 - jnp.where(lane < LANES // 2, at_right, at_left)
    ghost = jnp.where((lane == 0) & (row >= COND), at_right, 0.0)
    return halo * keep + pltpu.roll(last, 1, 1) * ghost


def step(state, weights, width, flags):
    columns = state.shape[1]
    pieces = []
    for b in range(0, columns, width):
        e = b + width
        pieces.append(state[:, b : e - LANES])
        pieces.append(fix_ends(state[:, e - 2 * LANES : e - LANES], state[:, e - LANES : e], flags))
    state = jnp.concatenate(pieces, axis=1)
    high = state.astype(jnp.bfloat16)
    low = (state - high.astype(jnp.float32)).astype(jnp.bfloat16)
    product = jnp.dot(
        weights,
        jnp.concatenate([high, high, low, high], axis=0),
        preferred_element_type=jnp.float32,
    )
    outs = []
    for b in range(0, columns, width):
        e = b + width
        here = product[:ROWS, b:e]
        from_left = pltpu.roll(product[ROWS : 2 * ROWS, b:e], 1, 1)
        from_right = pltpu.roll(product[2 * ROWS :, b:e], width - 1, 1)
        outs.append(
            jnp.concatenate(
                [here[:COND] + from_left[:COND], here[COND:] + from_left[COND:] + from_right], axis=0
            )
        )
    return outs[0] if len(outs) == 1 else jnp.concatenate(outs, axis=1)


def weights_kernel(blocks_ref, out_ref):
    p_v, k_v, p_i, k_i = (blocks_ref[m] for m in range(4))

    def product(a, b):
        return jnp.dot(
            a, b, precision=lax.Precision.HIGHEST, preferred_element_type=jnp.float32
        )

    kp = product(k_i, p_v)
    kk = product(k_i, k_v)
    zero = jnp.zeros_like(kk)
    rows = [[p_v, -k_v], [kp, p_i - 2.0 * kk], [zero, k_v], [zero, kk], [-kp, kk]]
    whole = jnp.concatenate([jnp.concatenate(r, axis=1) for r in rows], axis=0)
    high = whole.astype(jnp.bfloat16)
    rest = whole - high.astype(jnp.float32)
    low = rest.astype(jnp.bfloat16)
    least = (rest - low.astype(jnp.float32)).astype(jnp.bfloat16)
    out_ref[...] = jnp.concatenate([high, low, high, least], axis=1)


def make_weights(blocks):
    return pl.pallas_call(
        weights_kernel,
        out_shape=jax.ShapeDtypeStruct((5 * COND, 4 * ROWS), jnp.bfloat16),
        name="weights",
    )(blocks)


def edges_kernel(f_first, f_last, c_first, c_last, i_first, i_last, low_ref, high_ref):
    count = f_first.shape[0]
    for n in range(count):
        low_ref[n] = pack_edge(f_first[n], 0)
        high_ref[n] = pack_edge(f_last[n], LANES - REACH)
    low_ref[count] = pack_edge(c_first[0], 0)
    high_ref[count] = pack_edge(c_last[0], LANES - REACH)
    low_ref[count + 1] = pack_edge(i_first[...], 0)
    high_ref[count + 1] = pack_edge(i_last[...], LANES - REACH)


def cut_edges(forcing, c_guess, initial):
    count, _, length = forcing.shape
    end = length // LANES - 1

    def both(shape, at):
        return [pl.BlockSpec(shape, lambda g, a=a: at(a)) for a in (0, end)]

    shape = jax.ShapeDtypeStruct((count + 2, 8, LANES), jnp.float32)
    whole = pl.BlockSpec(shape.shape, lambda g: (0, 0, 0))
    return pl.pallas_call(
        edges_kernel,
        grid=(1,),
        out_shape=(shape, shape),
        in_specs=both((count, ROWS, LANES), lambda a: (0, 0, a))
        + both((1, ROWS, LANES), lambda a: (0, 0, a))
        + both((ROWS, LANES), lambda a: (0, a)),
        out_specs=(whole, whole),
        name="edges",
    )(forcing, forcing, c_guess, c_guess, initial, initial)


def write_parts(out_ref, main, halo, at):
    groups = out_ref.shape[0]
    length = main.shape[1]
    part = length // groups
    tiles = part // LANES

    def tile(k):
        if k < 0 or k == length // LANES:
            return halo
        return main[:, k * LANES : (k + 1) * LANES]

    for j in range(groups):
        for i in range(tiles):
            out_ref[j, at + ROWS * i : at + ROWS * (i + 1), :] = tile(j * tiles + i)
        rim = join_halo(tile((j + 1) * tiles), tile(j * tiles - 1))
        out_ref[j, at + ROWS * tiles : at + ROWS * tiles + COND, :] = pack_halo(rim)


def source_kernel(
    forcing_ref, guess_ref, initial_ref, left_ref, right_ref, weights_ref, out_ref, own_ref, state_ref
):
    n = pl.program_id(0)
    count = pl.num_programs(0)
    length = forcing_ref.shape[2]
    groups = out_ref.shape[0]
    part = length // groups
    tiles = part // LANES
    flags = end_flags(lax.axis_index("space"), lax.axis_size("space"))

    @pl.when(n == 0)
    def _():
        state_ref[...] = jnp.zeros_like(state_ref)

    state = step(state_ref[...], weights_ref[...], length + LANES, flags)
    main = state[:, :length] + forcing_ref[0]
    halo = state[:, length:] + halo_of_edges(left_ref[n], right_ref[n])
    state_ref[:, :length] = main
    state_ref[:, length:] = halo

    @pl.when(n == count - 1)
    def _():
        guess_halo = halo_of_edges(left_ref[count], right_ref[count])
        write_parts(out_ref, guess_ref[0], guess_halo, 0)
        write_parts(out_ref, state_ref[:, :length], state_ref[:, length:], tiles * ROWS + COND)
        j = lax.axis_index("tm")
        last = length // LANES - 1
        halo = halo_of_edges(left_ref[count + 1], right_ref[count + 1])

        def tile(k):
            inside = initial_ref[
                :, pl.ds(pl.multiple_of(jnp.clip(k, 0, last) * LANES, LANES), LANES)
            ]
            outside = jnp.where((k < 0) | (k > last), 1.0, 0.0).astype(jnp.float32)
            return inside * (1.0 - outside) + halo * outside

        own_ref[:, :part] = initial_ref[:, pl.ds(pl.multiple_of(j * part, LANES), part)]
        own_ref[:, part:] = join_halo(tile((j + 1) * tiles), tile(j * tiles - 1))


def source_chain(forcing, c_guess, initial, left, right, weights, groups):
    count, _, length = forcing.shape
    part = length // groups
    rows = 2 * (part // LANES * ROWS + COND)
    return pl.pallas_call(
        source_kernel,
        grid=(count,),
        out_shape=(
            jax.ShapeDtypeStruct((groups, rows, LANES), jnp.float32),
            jax.ShapeDtypeStruct((ROWS, part + LANES), jnp.float32),
        ),
        in_specs=[
            pl.BlockSpec((1, ROWS, length), lambda n: (n, 0, 0)),
            pl.BlockSpec((1, ROWS, length), lambda n: (0, 0, 0)),
            pl.BlockSpec((ROWS, length), lambda n: (0, 0)),
            pl.BlockSpec(left.shape, lambda n: (0, 0, 0)),
            pl.BlockSpec(right.shape, lambda n: (0, 0, 0)),
            pl.BlockSpec(weights.shape, lambda n: (0, 0)),
        ],
        out_specs=(
            pl.BlockSpec((groups, rows, LANES), lambda n: (0, 0, 0)),
            pl.BlockSpec((ROWS, part + LANES), lambda n: (0, 0)),
        ),
        scratch_shapes=[pltpu.VMEM((ROWS, length + LANES), jnp.float32)],
        compiler_params=pltpu.CompilerParams(vmem_limit_bytes=VMEM_LIMIT),
        name="source_chain",
    )(forcing, c_guess, initial, left, right, weights)


def coarse_kernel(parts_ref, own_ref, fine_ref, coarse_ref, out_ref, state_ref, value_ref):
    groups = parts_ref.shape[0]
    width = own_ref.shape[1]
    part = width - LANES
    tiles = part // LANES
    size = tiles * ROWS + COND
    space, spaces = lax.axis_index("space"), lax.axis_size("space")
    flags = end_flags(space * groups + lax.axis_index("tm"), spaces * groups)

    def ring(t, at):
        pieces = [parts_ref[t, at + ROWS * i : at + ROWS * (i + 1), :] for i in range(tiles)]
        pieces.append(unpack_halo(parts_ref[t, at + ROWS * tiles : at + size, :]))
        return jnp.concatenate(pieces, axis=1)

    def put(t, at, ring, rim):
        for i in range(tiles):
            out_ref[t, at + ROWS * i : at + ROWS * (i + 1), :] = ring[:, i * LANES : (i + 1) * LANES]
        if rim:
            out_ref[t, at + ROWS * tiles : at + size, :] = pack_halo(ring[:, part:])

    def cols(t):
        return slice(t * width, (t + 1) * width)

    def relax(columns):
        def one(i, carry):
            state_ref[:, :columns] = step(state_ref[:, :columns], fine_ref[...], width, flags)
            return carry

        lax.fori_loop(0, 8, one, 0)

    state_ref[:, cols(0)] = own_ref[...]
    for t in range(1, groups):
        state_ref[:, cols(t)] = ring(t - 1, 0)
    relax(groups * width)
    for t in range(groups):
        value_ref[:, cols(t)] = state_ref[:, cols(t)] + ring(t, size)

    for t in range(groups - 1):
        state_ref[:, cols(t)] = value_ref[:, cols(t)] - ring(t, 0)
    relax((groups - 1) * width)

    put(0, 0, own_ref[...], True)
    put(0, size, value_ref[:, cols(0)], False)
    correction = None
    for t in range(1, groups):
        resid = state_ref[:, cols(t - 1)]
        if correction is None:
            correction = resid
        else:
            correction = step(correction, coarse_ref[...], width, flags) + resid
        put(t, 0, value_ref[:, cols(t - 1)], True)
        put(t, size, value_ref[:, cols(t)] + correction, False)


def coarse_solve(parts, own, fine, coarse):
    groups, rows, _ = parts.shape
    width = own.shape[1]
    return pl.pallas_call(
        coarse_kernel,
        out_shape=jax.ShapeDtypeStruct((groups, rows - COND, LANES), jnp.float32),
        scratch_shapes=[
            pltpu.VMEM((ROWS, groups * width), jnp.float32),
            pltpu.VMEM((ROWS, groups * width), jnp.float32),
        ],
        compiler_params=pltpu.CompilerParams(vmem_limit_bytes=VMEM_LIMIT),
        name="coarse_solve",
    )(parts, own, fine, coarse)


def final_kernel(forcing_ref, parts_ref, left_ref, right_ref, weights_ref, out_ref, state_ref):
    n = pl.program_id(0)
    count = pl.num_programs(0)
    length = forcing_ref.shape[2]
    groups = parts_ref.shape[0]
    tiles = length // groups // LANES
    size = tiles * ROWS + COND
    flags = end_flags(lax.axis_index("space"), lax.axis_size("space"))

    def main(at):
        return jnp.concatenate(
            [
                parts_ref[j, at + ROWS * i : at + ROWS * (i + 1), :]
                for j in range(groups)
                for i in range(tiles)
            ],
            axis=1,
        )

    @pl.when(n == 0)
    def _():
        state_ref[:, :length] = main(0)
        state_ref[:, length:] = join_halo(
            unpack_halo(parts_ref[groups - 1, ROWS * tiles : size, :]),
            unpack_halo(parts_ref[0, ROWS * tiles : size, :]),
        )

    @pl.when(n < count - 1)
    def _():
        state = step(state_ref[...], weights_ref[...], length + LANES, flags)
        main = state[:, :length] + forcing_ref[0]
        state_ref[:, :length] = main
        state_ref[:, length:] = state[:, length:] + halo_of_edges(left_ref[n], right_ref[n])
        out_ref[0] = main

    @pl.when(n == count - 1)
    def _():
        out_ref[0] = main(size)


def final_chain(forcing, parts, left, right, weights):
    count, _, length = forcing.shape
    return pl.pallas_call(
        final_kernel,
        grid=(count,),
        out_shape=jax.ShapeDtypeStruct(forcing.shape, jnp.float32),
        in_specs=[
            pl.BlockSpec((1, ROWS, length), lambda n: (jnp.minimum(n, count - 2), 0, 0)),
            pl.BlockSpec(parts.shape, lambda n: (0, 0, 0)),
            pl.BlockSpec(left.shape, lambda n: (0, 0, 0)),
            pl.BlockSpec(right.shape, lambda n: (0, 0, 0)),
            pl.BlockSpec(weights.shape, lambda n: (0, 0)),
        ],
        out_specs=pl.BlockSpec((1, ROWS, length), lambda n: (n, 0, 0)),
        scratch_shapes=[pltpu.VMEM((ROWS, length + LANES), jnp.float32)],
        compiler_params=pltpu.CompilerParams(vmem_limit_bytes=VMEM_LIMIT),
        name="final_chain",
    )(forcing, parts, left, right, weights)


def body(initial, c_guess, forcing, fine_blocks, coarse_blocks):
    groups = lax.axis_size("tm")
    spaces = lax.axis_size("space")
    low, high = cut_edges(forcing, c_guess, initial)
    right = lax.ppermute(low, "space", [(i, (i - 1) % spaces) for i in range(spaces)])
    left = lax.ppermute(high, "space", [(i, (i + 1) % spaces) for i in range(spaces)])
    fine = make_weights(fine_blocks)
    coarse = make_weights(coarse_blocks)
    parts, own = source_chain(forcing, c_guess, initial, left, right, fine, groups)
    parts = lax.all_to_all(parts, "tm", 0, 0, tiled=True)
    parts = coarse_solve(parts, own, fine, coarse)
    parts = lax.all_to_all(parts, "tm", 0, 0, tiled=True)
    return final_chain(forcing, parts, left, right, fine)


def solution(mesh):
    in_specs = (P(None, "space"), P("tm", None, "space"), P("tm", None, "space"), P(), P())
    out_specs = P("tm", None, "space")
    return jax.shard_map(body, mesh=mesh, in_specs=in_specs, out_specs=out_specs, check_vma=False)
```

profile of v0, /device:TPU:104, one launch (start us, length us, event | category | flops | bytes accessed | tf_op | source)
XLA Modules:
  0.0 77.7 jit_solution(1002188527359531184)
XLA Ops:
  0.0 0.0 copy-start.1
  0.0 0.0 copy-start.2
  0.0 1.8 %edges.1 = (f32[10,8,128]{2,1,0:T(8,128)}, f32[10,8,128]{2,1,0:T(8,128)}) custom-call(f32[8,32,4096]{2,1,0:T(8,128)} %forcing_ref.3, f32[8,32,4096]{2,1,0:T(8,128)} %forcing_ref.3, f32[1,32,4096]{2,1,0:T(8,128)} %guess_ref.1, f32[1,32,4096]{2,1,0:T(8,128)} %guess_ref.1, f32[32,4096]{1,0:T(8,128)} %initial_ref.1, f32[32,4096]{1,0:T(8,128)} %initial_ref.1), custom_call_target="tpu_custom_call" | custom-call | tf_op jit(solution)/shard_map/edges/pallas_call | solution.py:146
  1.8 0.0 collective-permute-start
  1.8 1.7 %collective-permute-start.1 = (f32[10,8,128]{2,1,0:T(8,128)}, f32[10,8,128]{2,1,0:T(8,128)S(1)}, u32[]{:S(2)}, u32[]{:S(2)}) collective-permute-start(f32[10,8,128]{2,1,0:T(8,128)} %get-tuple-element.10), channel_id=1, source_target_pairs={{0,31},{1,0},{2,1},{3,2},{4,3},{5,4},{6,5},{7,6},{8,7},{9,8},{10,9... | collective-permute-start | bytes 122888 | tf_op jit(solution)/shard_map/ppermute | solution.py:379
  3.6 1.7 %weights.2.weights_ref.fine_ref = bf16[80,128]{1,0:T(8,128)(2,1)} custom-call(f32[4,16,16]{2,1,0:T(8,128)} %blocks_ref.2), custom_call_target="tpu_custom_call" | custom-call | tf_op jit(solution)/shard_map/weights/pallas_call | solution.py:119
  5.3 0.2 collective-permute-done.left_ref
  5.5 0.4 collective-permute-done.1.right_ref
  5.9 0.0 copy-done.1
  5.9 0.0 copy-done.2
  5.9 0.0 copy-start.3
  5.9 0.7 copy-done.3
  6.6 7.8 %source_chain.1 = (f32[8,288,128]{2,1,0:T(8,128)}, f32[32,640]{1,0:T(8,128)S(1)}) custom-call(f32[8,32,4096]{2,1,0:T(8,128)} %forcing_ref.3, f32[1,32,4096]{2,1,0:T(8,128)S(1)} %copy-done.1, f32[32,4096]{1,0:T(8,128)S(1)} %copy-done.2, f32[10,8,128]{2,1,0:T(8,128)S(1)} %collective-permute-done.left_ref, f32[10,8,128]{2,1,0:T(8,128)S(1)} %collective-permute-done.1.right_ref, ...), custom_call_target="tpu_custom_call" | custom-call | tf_op jit(solution)/shard_map/source_chain/pallas_call | solution.py:221
  14.4 0.0 copy-start.4
  14.4 6.5 %all-to-all-start = ((f32[8,288,128]{2,1,0:T(8,128)}), f32[8,288,128]{2,1,0:T(8,128)S(1)}, u32[]{:S(2)}, u32[]{:S(2)}) async-start(f32[8,288,128]{2,1,0:T(8,128)} %get-tuple-element.11), calls=%async_computation | async-start | bytes 2359296 | tf_op jit(solution)/shard_map/all_to_all | solution.py:384
  20.9 1.7 %weights.3.coarse_ref = bf16[80,128]{1,0:T(8,128)(2,1)} custom-call(f32[4,16,16]{2,1,0:T(8,128)} %blocks_ref.3), custom_call_target="tpu_custom_call" | custom-call | tf_op jit(solution)/shard_map/weights/pallas_call | solution.py:119
  22.5 17.9 %all-to-all-done.parts_ref = f32[8,288,128]{2,1,0:T(8,128)S(1)} async-done(((f32[8,288,128]{2,1,0:T(8,128)}), f32[8,288,128]{2,1,0:T(8,128)S(1)}, u32[]{:S(2)}, u32[]{:S(2)}) %all-to-all-start) | async-done | bytes 1179680 | tf_op jit(solution)/shard_map/all_to_all | solution.py:384
  40.4 0.0 copy-done.4
  40.4 0.0 copy-start.5
  40.4 0.7 copy-done.5
  41.1 0.0 copy-start
  41.2 10.1 %coarse_solve.1 = f32[8,272,128]{2,1,0:T(8,128)S(1)} custom-call(f32[8,288,128]{2,1,0:T(8,128)S(1)} %all-to-all-done.parts_ref, f32[32,640]{1,0:T(8,128)S(1)} %get-tuple-element.12.own_ref, bf16[80,128]{1,0:T(8,128)(2,1)S(1)} %copy-done.4, bf16[80,128]{1,0:T(8,128)(2,1)S(1)} %copy-done.5), custom_call_target="tpu_custom_call" | custom-call | tf_op jit(solution)/shard_map/coarse_solve/pallas_call | solution.py:303
  51.3 21.2 %all_to_all.10.parts_ref = f32[8,272,128]{2,1,0:T(8,128)S(1)} all-to-all(f32[8,272,128]{2,1,0:T(8,128)S(1)} %coarse_solve.1), channel_id=1, replica_groups=mesh['tm'=8,'space'=32] {'tm'}, dimensions={0} | all-to-all | bytes 2228224 | tf_op jit(solution)/shard_map/all_to_all | solution.py:386
  72.5 0.0 copy-done
  72.5 5.2 %final_chain.1 = f32[8,32,4096]{2,1,0:T(8,128)} custom-call(f32[8,32,4096]{2,1,0:T(8,128)S(1)} %copy-done, f32[8,272,128]{2,1,0:T(8,128)S(1)} %all_to_all.10.parts_ref, f32[10,8,128]{2,1,0:T(8,128)S(1)} %collective-permute-done.left_ref, f32[10,8,128]{2,1,0:T(8,128)S(1)} %collective-permute-done.1.right_ref, bf16[80,128]{1,0:T(8,128)(2,1)S(1)} %copy-done.4), custom_call_target="tpu_custom_call" | custom-call | tf_op jit(solution)/shard_map/final_chain/pallas_call | solution.py:357
Async XLA Ops:
  0.0 5.9 %copy-start.1 = (f32[1,32,4096]{2,1,0:T(8,128)S(1)}, f32[1,32,4096]{2,1,0:T(8,128)}, u32[]{:S(2)}) copy-start(f32[1,32,4096]{2,1,0:T(8,128)} %guess_ref.1) | copy-start | bytes 1572868
  0.0 5.9 %copy-start.2 = (f32[32,4096]{1,0:T(8,128)S(1)}, f32[32,4096]{1,0:T(8,128)}, u32[]{:S(2)}) copy-start(f32[32,4096]{1,0:T(8,128)} %initial_ref.1) | copy-start | bytes 1572868
  1.8 3.6 %collective-permute-start = (f32[10,8,128]{2,1,0:T(8,128)}, f32[10,8,128]{2,1,0:T(8,128)S(1)}, u32[]{:S(2)}, u32[]{:S(2)}) collective-permute-start(f32[10,8,128]{2,1,0:T(8,128)} %get-tuple-element.9), channel_id=1, source_target_pairs={{0,1},{1,2},{2,3},{3,4},{4,5},{5,6},{6,7},{7,8},{8,9},{9,10},{10,1... | collective-permute-start | bytes 122888 | tf_op jit(solution)/shard_map/ppermute | solution.py:380
  1.8 4.0 %collective-permute-start.1 = (f32[10,8,128]{2,1,0:T(8,128)}, f32[10,8,128]{2,1,0:T(8,128)S(1)}, u32[]{:S(2)}, u32[]{:S(2)}) collective-permute-start(f32[10,8,128]{2,1,0:T(8,128)} %get-tuple-element.10), channel_id=1, source_target_pairs={{0,31},{1,0},{2,1},{3,2},{4,3},{5,4},{6,5},{7,6},{8,7},{9,8},{10,9... | collective-permute-start | bytes 122888 | tf_op jit(solution)/shard_map/ppermute | solution.py:379
  5.9 0.7 copy-start.3
  14.4 26.0 %copy-start.4 = (bf16[80,128]{1,0:T(8,128)(2,1)S(1)}, bf16[80,128]{1,0:T(8,128)(2,1)}, u32[]{:S(2)}) copy-start(bf16[80,128]{1,0:T(8,128)(2,1)} %weights.2.weights_ref.fine_ref) | copy-start | bytes 61444
  14.4 26.0 %all-to-all-start = ((f32[8,288,128]{2,1,0:T(8,128)}), f32[8,288,128]{2,1,0:T(8,128)S(1)}, u32[]{:S(2)}, u32[]{:S(2)}) async-start(f32[8,288,128]{2,1,0:T(8,128)} %get-tuple-element.11), calls=%async_computation | async-start | bytes 2359296 | tf_op jit(solution)/shard_map/all_to_all | solution.py:384
  40.4 0.7 copy-start.5
  41.1 31.3 %copy-start = (f32[8,32,4096]{2,1,0:T(8,128)S(1)}, f32[8,32,4096]{2,1,0:T(8,128)}, u32[]{:S(2)}) copy-start(f32[8,32,4096]{2,1,0:T(8,128)} %forcing_ref.3) | copy-start | bytes 12582916
where the time goes:
time: 78.8 us; the launch traced here: 77.7 us
  Pallas kernels  28.3 us (36%)
  blocking collectives  21.2 us (27%)
  waiting for transfers between devices  18.5 us (23%)
  starting transfers between devices  8.2 us (10%)
  local copies, waits for them, and re-layouts  1.47 us (2%)
    all_to_all x1, blocking collectives, body(): parts = lax.all_to_all(parts, 'tm', 0, 0, tiled=True)  21.2 us
    all_to_all x1, waiting for transfers between devices, body(): parts = lax.all_to_all(parts, 'tm', 0, 0, tiled=True)  17.9 us
    pallas_call x1, Pallas kernels, coarse_solve(): pl.pallas_call(coarse_kernel, out_shape=jax.ShapeDtypeStruct((groups, row...  10.1 us
    pallas_call x1, Pallas kernels, source_chain(): pl.pallas_call(source_kernel, grid=(count,), out_shape=(jax.ShapeDtypeStr...  7.77 us
    all_to_all x1, starting transfers between devices, body(): parts = lax.all_to_all(parts, 'tm', 0, 0, tiled=True)  6.45 us
    pallas_call x1, Pallas kernels, final_chain(): pl.pallas_call(final_kernel, grid=(count,), out_shape=jax.ShapeDtypeStruc...  5.23 us
    pallas_call x2, Pallas kernels, make_weights(): pl.pallas_call(weights_kernel, out_shape=jax.ShapeDtypeStruct((5 * COND,...  3.32 us
    pallas_call x1, Pallas kernels, cut_edges(): pl.pallas_call(edges_kernel, grid=(1,), out_shape=(shape, shape), in_spec...  1.84 us
  transfers between devices with their start and end apart: 3, of which 3 were waited for; matrix products, arithmetic and copies ran while one was open for 0% of the time, Pallas kernels for 4%

commit v1 on v0

v1 whole, which is shorter than its diff:
```python
import jax
import jax.numpy as jnp
from jax import lax
from jax.experimental import pallas as pl
from jax.experimental.pallas import tpu as pltpu
from jax.sharding import PartitionSpec as P

LANES = 128
REACH = 32
COND = 16
ROWS = 2 * COND
VMEM_LIMIT = 20 * 1024 * 1024


def iota(shape, axis):
    return lax.broadcasted_iota(jnp.int32, shape, axis)


def pack_edge(tile, base):
    lane = iota((8, LANES), 1)
    out = jnp.zeros((8, LANES), jnp.float32)
    for g in range(4):
        part = pltpu.roll(tile[8 * g : 8 * g + 8], (REACH * g - base) % LANES, 1)
        out = jnp.where(lane // REACH == g, part, out)
    return out


def unpack_edge(packed, base):
    return jnp.concatenate(
        [pltpu.roll(packed, (base - REACH * g) % LANES, 1) for g in range(4)], axis=0
    )


def halo_of_edges(from_left, from_right):
    lane = iota((ROWS, LANES), 1)
    right = jnp.where(lane < REACH, unpack_edge(from_right, 0), 0.0)
    return jnp.where(lane >= LANES - REACH, unpack_edge(from_left, LANES - REACH), right)


def pack_halo(halo):
    lane = iota((COND, LANES), 1)
    outer = (lane < REACH) | (lane >= LANES - REACH)
    return jnp.where(outer, halo[:COND], pltpu.roll(halo[COND:], LANES // 2, 1))


def unpack_halo(packed):
    return jnp.concatenate([packed, pltpu.roll(packed, LANES // 2, 1)], axis=0)


def join_halo(right, left):
    return jnp.where(iota((ROWS, LANES), 1) < LANES // 2, right, left)


def end_flags(index, size):
    at_left = jnp.where(index == 0, 1.0, 0.0).astype(jnp.float32)
    at_right = jnp.where(index == size - 1, 1.0, 0.0).astype(jnp.float32)
    return at_left, at_right


def fix_ends(last, halo, flags):
    at_left, at_right = flags
    lane = iota((ROWS, LANES), 1)
    row = iota((ROWS, LANES), 0)
    keep = 1.0 - jnp.where(lane < LANES // 2, at_right, at_left)
    ghost = jnp.where((lane == 0) & (row >= COND), at_right, 0.0)
    return halo * keep + pltpu.roll(last, 1, 1) * ghost


def step(state, weights, width, flags):
    columns = state.shape[1]
    pieces = []
    for b in range(0, columns, width):
        e = b + width
        pieces.append(state[:, b : e - LANES])
        pieces.append(fix_ends(state[:, e - 2 * LANES : e - LANES], state[:, e - LANES : e], flags))
    state = jnp.concatenate(pieces, axis=1)
    high = state.astype(jnp.bfloat16)
    low = (state - high.astype(jnp.float32)).astype(jnp.bfloat16)
    product = jnp.dot(
        weights,
        jnp.concatenate([high, high, low, high], axis=0),
        preferred_element_type=jnp.float32,
    )
    outs = []
    for b in range(0, columns, width):
        e = b + width
        here = product[:ROWS, b:e]
        from_left = pltpu.roll(product[ROWS : 2 * ROWS, b:e], 1, 1)
        from_right = pltpu.roll(product[2 * ROWS :, b:e], width - 1, 1)
        outs.append(
            jnp.concatenate(
                [here[:COND] + from_left[:COND], here[COND:] + from_left[COND:] + from_right], axis=0
            )
        )
    return outs[0] if len(outs) == 1 else jnp.concatenate(outs, axis=1)


def prepare_kernel(fine_ref, coarse_ref, forcing_ref, out_ref, staged_ref, sem):
    copy = pltpu.make_async_copy(forcing_ref, staged_ref, sem)
    copy.start()

    def product(a, b):
        return jnp.dot(
            a, b, precision=lax.Precision.HIGHEST, preferred_element_type=jnp.float32
        )

    for m, blocks_ref in enumerate((fine_ref, coarse_ref)):
        p_v, k_v, p_i, k_i = (blocks_ref[r] for r in range(4))
        kp = product(k_i, p_v)
        kk = product(k_i, k_v)
        zero = jnp.zeros_like(kk)
        rows = [[p_v, -k_v], [kp, p_i - 2.0 * kk], [zero, k_v], [zero, kk], [-kp, kk]]
        whole = jnp.concatenate([jnp.concatenate(r, axis=1) for r in rows], axis=0)
        high = whole.astype(jnp.bfloat16)
        rest = whole - high.astype(jnp.float32)
        low = rest.astype(jnp.bfloat16)
        least = (rest - low.astype(jnp.float32)).astype(jnp.bfloat16)
        out_ref[m] = jnp.concatenate([high, low, high, least], axis=1)
    copy.wait()


def prepare(fine_blocks, coarse_blocks, forcing):
    vmem = pl.BlockSpec(memory_space=pltpu.VMEM)
    return pl.pallas_call(
        prepare_kernel,
        out_shape=(
            pltpu.VMEM((2, 5 * COND, 4 * ROWS), jnp.bfloat16),
            pltpu.VMEM(forcing.shape, jnp.float32),
        ),
        in_specs=[vmem, vmem, pl.BlockSpec(memory_space=pltpu.HBM)],
        out_specs=(vmem, vmem),
        scratch_shapes=[pltpu.SemaphoreType.DMA],
        compiler_params=pltpu.CompilerParams(vmem_limit_bytes=VMEM_LIMIT),
        name="prepare",
    )(fine_blocks, coarse_blocks, pltpu.with_memory_space_constraint(forcing, pltpu.HBM))


def edges_kernel(
    f_first, f_last, c_first, c_last, i_first, i_last, low_ref, high_ref, low_guess_ref, high_guess_ref
):
    count = f_first.shape[0]
    for n in range(count):
        low_ref[n] = pack_edge(f_first[n], 0)
        high_ref[n] = pack_edge(f_last[n], LANES - REACH)
    low_guess_ref[...] = pack_edge(c_first[0], 0)
    high_guess_ref[...] = pack_edge(c_last[0], LANES - REACH)
    low_ref[count] = low_guess_ref[...]
    high_ref[count] = high_guess_ref[...]
    low_ref[count + 1] = pack_edge(i_first[...], 0)
    high_ref[count + 1] = pack_edge(i_last[...], LANES - REACH)


def cut_edges(forcing, c_guess, initial):
    count, _, length = forcing.shape
    end = length // LANES - 1

    def both(shape, at):
        return [pl.BlockSpec(shape, lambda g, a=a: at(a)) for a in (0, end)]

    shape = jax.ShapeDtypeStruct((count + 2, 8, LANES), jnp.float32)
    whole = pl.BlockSpec(shape.shape, lambda g: (0, 0, 0))
    guess = jax.ShapeDtypeStruct((8, LANES), jnp.float32)
    whole_guess = pl.BlockSpec(guess.shape, lambda g: (0, 0))
    return pl.pallas_call(
        edges_kernel,
        grid=(1,),
        out_shape=(shape, shape, guess, guess),
        in_specs=both((count, ROWS, LANES), lambda a: (0, 0, a))
        + both((1, ROWS, LANES), lambda a: (0, 0, a))
        + both((ROWS, LANES), lambda a: (0, a)),
        out_specs=(whole, whole, whole_guess, whole_guess),
        name="edges",
    )(forcing, forcing, c_guess, c_guess, initial, initial)


def write_parts(out_ref, main, halo, at):
    groups = out_ref.shape[0]
    length = main.shape[1]
    part = length // groups
    tiles = part // LANES

    def tile(k):
        if k < 0 or k == length // LANES:
            return halo
        return main[:, k * LANES : (k + 1) * LANES]

    for j in range(groups):
        for i in range(tiles):
            out_ref[j, at + ROWS * i : at + ROWS * (i + 1), :] = tile(j * tiles + i)
        rim = join_halo(tile((j + 1) * tiles), tile(j * tiles - 1))
        out_ref[j, at + ROWS * tiles : at + ROWS * tiles + COND, :] = pack_halo(rim)


def start_chain(main_ref, halo_ref, begin_ref, initial_ref, left_ref, right_ref, sem):
    is_first = lax.axis_index("tm") == 0
    last = left_ref.shape[0] - 1

    @pl.when(is_first)
    def _():
        pltpu.make_async_copy(initial_ref, main_ref, sem).start()
        halo_ref[...] = halo_of_edges(left_ref[last], right_ref[last])

    @pl.when(jnp.logical_not(is_first))
    def _():
        pltpu.make_async_copy(begin_ref, main_ref, sem).start()

    return pltpu.make_async_copy(begin_ref, main_ref, sem)


def advance(main, halo, source, left, right, weights, flags):
    length = main.shape[1]
    state = step(jnp.concatenate([main, halo], axis=1), weights, length + LANES, flags)
    return state[:, :length] + source, state[:, length:] + halo_of_edges(left, right)


def first_kernel(
    forcing_ref,
    begin_ref,
    initial_ref,
    guess_ref,
    left_ref,
    right_ref,
    begin_left_ref,
    begin_right_ref,
    weights_ref,
    out_ref,
    value_ref,
    own_ref,
    sems,
):
    count = forcing_ref.shape[0]
    length = forcing_ref.shape[2]
    flags = end_flags(lax.axis_index("space"), lax.axis_size("space"))
    main_ref, halo_ref = value_ref.at[:, :length], value_ref.at[:, length:]

    halo_ref[...] = halo_of_edges(begin_left_ref[...], begin_right_ref[...])
    begun = start_chain(
        main_ref, halo_ref, begin_ref, initial_ref, left_ref, right_ref, sems.at[0]
    )
    own = pltpu.make_async_copy(guess_ref.at[0], own_ref, sems.at[1])
    own.start()
    begun.wait()

    def one(n, carry):
        main, halo = advance(
            main_ref[...],
            halo_ref[...],
            forcing_ref[n],
            left_ref[n],
            right_ref[n],
            weights_ref[0],
            flags,
        )
        main_ref[...] = main
        halo_ref[...] = halo
        return carry

    lax.fori_loop(0, count, one, 0)
    own.wait()
    guess_halo = halo_of_edges(left_ref[count], right_ref[count])
    write_parts(out_ref, main_ref[...] - own_ref[...], halo_ref[...] - guess_halo, 0)


def first_chain(
    forcing, begin, initial, c_guess, left, right, begin_left, begin_right, weights, groups
):
    count, _, length = forcing.shape
    rows = length // groups // LANES * ROWS + COND
    anywhere = pl.BlockSpec(memory_space=pl.ANY)
    vmem = pl.BlockSpec(memory_space=pltpu.VMEM)
    return pl.pallas_call(
        first_kernel,
        out_shape=(
            jax.ShapeDtypeStruct((groups, rows, LANES), jnp.float32),
            jax.ShapeDtypeStruct((ROWS, length + LANES), jnp.float32),
        ),
        in_specs=[vmem, anywhere, anywhere, anywhere, vmem, vmem, vmem, vmem, vmem],
        out_specs=(vmem, vmem),
        scratch_shapes=[
            pltpu.VMEM((ROWS, length), jnp.float32),
            pltpu.SemaphoreType.DMA((2,)),
        ],
        compiler_params=pltpu.CompilerParams(vmem_limit_bytes=VMEM_LIMIT),
        cost_estimate=cost(count, length, forcing.size),
        name="first_chain",
    )(forcing, begin, initial, c_guess, left, right, begin_left, begin_right, weights)


def cost(steps, columns, elements):
    return pl.CostEstimate(
        flops=steps * columns * 80 * 128 * 16, bytes_accessed=8 * elements, transcendentals=0
    )


def coarse_kernel(parts_ref, weights_ref, out_ref, state_ref):
    groups = parts_ref.shape[0]
    tiles = (parts_ref.shape[1] - COND) // ROWS
    part = tiles * LANES
    width = part + LANES
    space, spaces = lax.axis_index("space"), lax.axis_size("space")
    flags = end_flags(space * groups + lax.axis_index("tm"), spaces * groups)

    def cols(t):
        return slice(t * width, (t + 1) * width)

    for t in range(groups - 1):
        for i in range(tiles):
            at = t * width + i * LANES
            state_ref[:, at : at + LANES] = parts_ref[t, ROWS * i : ROWS * (i + 1), :]
        state_ref[:, t * width + part : (t + 1) * width] = unpack_halo(
            parts_ref[t, ROWS * tiles : ROWS * tiles + COND, :]
        )

    def one(i, carry):
        state_ref[...] = step(state_ref[...], weights_ref[0], width, flags)
        return carry

    lax.fori_loop(0, 8, one, 0)

    out_ref[0] = jnp.zeros_like(out_ref[0])
    correction = None
    for t in range(1, groups):
        resid = state_ref[:, cols(t - 1)]
        if correction is None:
            correction = resid
        else:
            correction = step(correction, weights_ref[1], width, flags) + resid
        for i in range(tiles):
            out_ref[t, ROWS * i : ROWS * (i + 1), :] = correction[:, i * LANES : (i + 1) * LANES]


def coarse_solve(parts, weights):
    groups, rows, _ = parts.shape
    tiles = (rows - COND) // ROWS
    return pl.pallas_call(
        coarse_kernel,
        out_shape=jax.ShapeDtypeStruct((groups, ROWS * tiles, LANES), jnp.float32),
        scratch_shapes=[pltpu.VMEM((ROWS, (groups - 1) * (tiles + 1) * LANES), jnp.float32)],
        compiler_params=pltpu.CompilerParams(vmem_limit_bytes=VMEM_LIMIT),
        cost_estimate=cost(12, groups * tiles * LANES, parts.size),
        name="coarse_solve",
    )(parts, weights)


def second_kernel(
    forcing_ref,
    begin_ref,
    initial_ref,
    left_ref,
    right_ref,
    weights_ref,
    out_ref,
    states_ref,
    halo_ref,
    sems,
    out_sems,
):
    steps = out_sems.shape[0]
    length = forcing_ref.shape[2]
    flags = end_flags(lax.axis_index("space"), lax.axis_size("space"))

    halo = pltpu.make_async_copy(begin_ref.at[:, length:], halo_ref, sems.at[1])
    halo.start()
    halo.wait()
    begun = start_chain(
        states_ref.at[0],
        halo_ref,
        begin_ref.at[:, :length],
        initial_ref,
        left_ref,
        right_ref,
        sems.at[0],
    )

    def result(n):
        return pltpu.make_async_copy(states_ref.at[n + 1], out_ref.at[n], out_sems.at[n])

    begun.wait()

    def one(n, carry):
        main, halo = advance(
            states_ref[n],
            halo_ref[...],
            forcing_ref[n],
            left_ref[n],
            right_ref[n],
            weights_ref[0],
            flags,
        )
        states_ref[n + 1] = main
        halo_ref[...] = halo
        result(n).start()
        return carry

    lax.fori_loop(0, steps, one, 0)
    for n in range(steps):
        result(n).wait()


def second_chain(forcing, begin, initial, left, right, weights):
    count, _, length = forcing.shape
    hbm = pl.BlockSpec(memory_space=pltpu.HBM)
    anywhere = pl.BlockSpec(memory_space=pl.ANY)
    vmem = pl.BlockSpec(memory_space=pltpu.VMEM)
    return pl.pallas_call(
        second_kernel,
        out_shape=jax.ShapeDtypeStruct(forcing.shape, jnp.float32),
        in_specs=[vmem, anywhere, anywhere, vmem, vmem, vmem],
        out_specs=hbm,
        scratch_shapes=[
            pltpu.VMEM(forcing.shape, jnp.float32),
            pltpu.VMEM((ROWS, LANES), jnp.float32),
            pltpu.SemaphoreType.DMA((2,)),
            pltpu.SemaphoreType.DMA((count - 1,)),
        ],
        compiler_params=pltpu.CompilerParams(vmem_limit_bytes=VMEM_LIMIT),
        cost_estimate=cost(count, length, 2 * forcing.size),
        name="second_chain",
    )(forcing, begin, initial, left, right, weights)


def correct_kernel(value_ref, parts_ref, states_ref, out_ref):
    del states_ref
    groups = parts_ref.shape[0]
    tiles = out_ref.shape[2] // groups // LANES
    for j in range(groups):
        for i in range(tiles):
            at = (j * tiles + i) * LANES
            out_ref[0, :, at : at + LANES] = (
                value_ref[:, at : at + LANES] + parts_ref[j, ROWS * i : ROWS * (i + 1), :]
            )


def correct_last(value, parts, states):
    count, _, length = states.shape
    return pl.pallas_call(
        correct_kernel,
        grid=(1,),
        out_shape=jax.ShapeDtypeStruct(states.shape, jnp.float32),
        in_specs=[
            pl.BlockSpec(value.shape, lambda g: (0, 0)),
            pl.BlockSpec(parts.shape, lambda g: (0, 0, 0)),
            pl.BlockSpec(memory_space=pl.ANY),
        ],
        out_specs=pl.BlockSpec((1, ROWS, length), lambda g: (count - 1, 0, 0)),
        input_output_aliases={2: 0},
        compiler_params=pltpu.CompilerParams(vmem_limit_bytes=VMEM_LIMIT),
        name="correct_last",
    )(value, parts, states)


def body(initial, c_guess, forcing, fine_blocks, coarse_blocks):
    groups = lax.axis_size("tm")
    spaces = lax.axis_size("space")
    up = [(i, (i + 1) % spaces) for i in range(spaces)]
    down = [(b, a) for a, b in up]
    to_next = [(i, (i + 1) % groups) for i in range(groups)]

    def to_next_and(pairs):
        return [(t * spaces + a, u * spaces + b) for t, u in to_next for a, b in pairs]

    begin = lax.ppermute(c_guess[0], "tm", to_next)
    low, high, low_guess, high_guess = cut_edges(forcing, c_guess, initial)
    right = lax.ppermute(low, "space", down)
    left = lax.ppermute(high, "space", up)
    begin_right = lax.ppermute(low_guess, ("tm", "space"), to_next_and(down))
    begin_left = lax.ppermute(high_guess, ("tm", "space"), to_next_and(up))
    weights, staged = prepare(fine_blocks, coarse_blocks, forcing)
    parts, value = first_chain(
        staged, begin, initial, c_guess, left, right, begin_left, begin_right, weights, groups
    )
    parts = lax.all_to_all(parts, "tm", 0, 0, tiled=True)
    begin = lax.ppermute(value, "tm", to_next)
    parts = coarse_solve(parts, weights)
    parts = lax.all_to_all(parts, "tm", 0, 0, tiled=True)
    states = second_chain(staged, begin, initial, left, right, weights)
    return correct_last(value, parts, states)


def solution(mesh):
    in_specs = (P(None, "space"), P("tm", None, "space"), P("tm", None, "space"), P(), P())
    out_specs = P("tm", None, "space")
    return jax.shard_map(body, mesh=mesh, in_specs=in_specs, out_specs=out_specs, check_vma=False)
```

time: 78.8 us -> 64.3 us (0.82)
  blocking collectives: 21.2 us -> 0 us
  Pallas kernels: 28.3 us -> 20.4 us
  starting transfers between devices: 8.2 us -> 15.6 us
  waiting for transfers between devices: 18.5 us -> 25.7 us
    all_to_all x1 -> x0, blocking collectives: 21.2 us -> none  [body(): parts = lax.all_to_all(parts, 'tm', 0, 0, tiled=True)]
    ppermute x2 -> x6, waiting for transfers between devices: 0.64 us -> 9.45 us  [the longest x1 4.36 us: body(): begin_left = lax.ppermute(high_guess, ('tm', 'space'), to_next_and(up))]
    pallas_call x6, Pallas kernels: 28.3 us -> 20.4 us  [the longest x1 6.58 us: coarse_solve(): pl.pallas_call(coarse_kernel, out_shape=jax.ShapeDtypeStruct((groups, ROW...]
    ppermute x2 -> x6, starting transfers between devices: 1.75 us -> 8.53 us  [the longest x1 2.48 us: body(): begin_left = lax.ppermute(high_guess, ('tm', 'space'), to_next_and(up))]
    all_to_all x1 -> x2, waiting for transfers between devices: 17.9 us -> 16.2 us  [body(): parts = lax.all_to_all(parts, 'tm', 0, 0, tiled=True)]
    all_to_all x1 -> x2, starting transfers between devices: 6.45 us -> 7.04 us  [body(): parts = lax.all_to_all(parts, 'tm', 0, 0, tiled=True)]
  transfers between devices with their start and end apart: 3 -> 8, of which waited for: 3 -> 6; matrix products, arithmetic and copies ran while one was open for 0% -> 0% of each run, Pallas kernels for 4% -> 23%
where the time goes in v1:
time: 64.3 us; the launch traced here: 64 us
  waiting for transfers between devices  25.7 us (40%)
  Pallas kernels  20.4 us (32%)
  starting transfers between devices  15.6 us (24%)
  local copies, waits for them, and re-layouts  2.21 us (3%)
    all_to_all x2, waiting for transfers between devices, body(): parts = lax.all_to_all(parts, 'tm', 0, 0, tiled=True)  16.2 us
    all_to_all x2, starting transfers between devices, body(): parts = lax.all_to_all(parts, 'tm', 0, 0, tiled=True)  7.04 us
    pallas_call x1, Pallas kernels, coarse_solve(): pl.pallas_call(coarse_kernel, out_shape=jax.ShapeDtypeStruct((groups, ROW...  6.58 us
    pallas_call x1, Pallas kernels, first_chain(): pl.pallas_call(first_kernel, out_shape=(jax.ShapeDtypeStruct((groups, row...  4.85 us
    ppermute x1, waiting for transfers between devices, body(): begin_left = lax.ppermute(high_guess, ('tm', 'space'), to_next_and(up))  4.36 us
    pallas_call x1, Pallas kernels, second_chain(): pl.pallas_call(second_kernel, out_shape=jax.ShapeDtypeStruct(forcing.shap...  4.17 us
    ppermute x1, starting transfers between devices, body(): begin_left = lax.ppermute(high_guess, ('tm', 'space'), to_next_and(up))  2.48 us
    unnamed x12, local copies, waits for them, and re-layouts  2.21 us
  transfers between devices with their start and end apart: 8, of which 6 were waited for; matrix products, arithmetic and copies ran while one was open for 0% of the time, Pallas kernels for 23%

profile of v1, /device:TPU:104, one launch (start us, length us, event | category | flops | bytes accessed | tf_op | source)
XLA Modules:
  0.0 64.0 jit_solution(9131856305146501708)
XLA Ops:
  0.0 0.0 copy-start.2
  0.0 0.0 copy-start.3
  0.0 1.5 %collective-permute-start = (f32[32,4096]{1,0:T(8,128)}, f32[32,4096]{1,0:T(8,128)S(1)}, u32[]{:S(2)}, u32[]{:S(2)}) collective-permute-start(f32[32,4096]{1,0:T(8,128)} %bitcast.1), channel_id=1, source_target_pairs={{0,32},{32,64},{64,96},{96,128},{128,160},{160,192},{192,224},{224... | collective-permute-start | bytes 1572872 | tf_op jit(solution)/shard_map/ppermute | solution.py:462
  1.5 1.8 %edges.1 = (f32[10,8,128]{2,1,0:T(8,128)}, f32[10,8,128]{2,1,0:T(8,128)}, f32[8,128]{1,0:T(8,128)}, f32[8,128]{1,0:T(8,128)}) custom-call(f32[8,32,4096]{2,1,0:T(8,128)} %f_last.1, f32[8,32,4096]{2,1,0:T(8,128)} %f_last.1, f32[1,32,4096]{2,1,0:T(8,128)} %guess_ref.1, f32[1,32,4096]{2,1,0:T(8,128)} %guess_ref.1, f32[32,4096]{1,0:T(8,128)} %initial_ref.3, ...), custom_call_target="tpu_custom_call" | custom-call | tf_op jit(solution)/shard_map/edges/pallas_call | solution.py:164
  3.3 0.0 copy-start
  3.3 0.0 copy-start.1
  3.3 0.1 collective-permute-start.1
  3.4 1.7 %collective-permute-start.2 = (f32[10,8,128]{2,1,0:T(8,128)}, f32[10,8,128]{2,1,0:T(8,128)S(1)}, u32[]{:S(2)}, u32[]{:S(2)}) collective-permute-start(f32[10,8,128]{2,1,0:T(8,128)} %get-tuple-element.15), channel_id=1, source_target_pairs={{1,0},{2,1},{3,2},{4,3},{5,4},{6,5},{7,6},{8,7},{9,8},{10,9},{11,1... | collective-permute-start | bytes 122888 | tf_op jit(solution)/shard_map/ppermute | solution.py:464
  5.1 2.5 %collective-permute-start.3 = (f32[8,128]{1,0:T(8,128)}, f32[8,128]{1,0:T(8,128)S(1)}, u32[]{:S(2)}, u32[]{:S(2)}) collective-permute-start(f32[8,128]{1,0:T(8,128)} %get-tuple-element.16), channel_id=1, source_target_pairs={{0,33},{1,34},{2,35},{3,36},{4,37},{5,38},{6,39},{7,40},{8,41},{9,... | collective-permute-start | bytes 12296 | tf_op jit(solution)/shard_map/ppermute | solution.py:467
  7.6 0.8 %collective-permute-start.4 = (f32[8,128]{1,0:T(8,128)}, f32[8,128]{1,0:T(8,128)S(1)}, u32[]{:S(2)}, u32[]{:S(2)}) collective-permute-start(f32[8,128]{1,0:T(8,128)} %get-tuple-element.17), channel_id=1, source_target_pairs={{1,32},{2,33},{3,34},{4,35},{5,36},{6,37},{7,38},{8,39},{9,40},{10... | collective-permute-start | bytes 12296 | tf_op jit(solution)/shard_map/ppermute | solution.py:466
  8.4 0.0 copy-done.2
  8.4 0.0 copy-done.3
  8.4 2.2 %prepare.1 = (bf16[2,80,128]{2,1,0:T(8,128)(2,1)S(1)}, f32[8,32,4096]{2,1,0:T(8,128)S(1)}) custom-call(f32[4,16,16]{2,1,0:T(8,128)S(1)} %copy-done.2, f32[4,16,16]{2,1,0:T(8,128)S(1)} %copy-done.3, f32[8,32,4096]{2,1,0:T(8,128)} %f_last.1), custom_call_target="tpu_custom_call" | custom-call | tf_op jit(solution)/shard_map/prepare/pallas_call | solution.py:124
  10.6 0.0 copy-start.4
  10.6 4.4 %collective-permute-done.3.begin_left_ref = f32[8,128]{1,0:T(8,128)S(1)} collective-permute-done((f32[8,128]{1,0:T(8,128)}, f32[8,128]{1,0:T(8,128)S(1)}, u32[]{:S(2)}, u32[]{:S(2)}) %collective-permute-start.3) | collective-permute-done | bytes 4128 | tf_op jit(solution)/shard_map/ppermute | solution.py:467
  15.0 2.1 %collective-permute-done.4.begin_right_ref = f32[8,128]{1,0:T(8,128)S(1)} collective-permute-done((f32[8,128]{1,0:T(8,128)}, f32[8,128]{1,0:T(8,128)S(1)}, u32[]{:S(2)}, u32[]{:S(2)}) %collective-permute-start.4) | collective-permute-done | bytes 4128 | tf_op jit(solution)/shard_map/ppermute | solution.py:466
  17.0 1.5 %collective-permute-done.1.left_ref = f32[10,8,128]{2,1,0:T(8,128)S(1)} collective-permute-done((f32[10,8,128]{2,1,0:T(8,128)}, f32[10,8,128]{2,1,0:T(8,128)S(1)}, u32[]{:S(2)}, u32[]{:S(2)}) %collective-permute-start.1) | collective-permute-done | bytes 40992 | tf_op jit(solution)/shard_map/ppermute | solution.py:465
  18.6 0.0 collective-permute-done.2.right_ref
  18.6 0.0 collective-permute-done.begin_ref
  18.6 0.0 copy-done
  18.6 0.0 copy-done.1
  18.6 4.8 %first_chain.1 = (f32[8,144,128]{2,1,0:T(8,128)}, f32[32,4224]{1,0:T(8,128)S(1)}) custom-call(f32[8,32,4096]{2,1,0:T(8,128)S(1)} %get-tuple-element.13.forcing_ref, f32[32,4096]{1,0:T(8,128)S(1)} %collective-permute-done.begin_ref, f32[32,4096]{1,0:T(8,128)S(1)} %copy-done.1, f32[1,32,4096]{2,1,0:T(8,128)S(1)} %copy-done, ...), custom_call_target="tpu_custom_call" | custom-call | flops 5368709120 | bytes 8388608 | tf_op jit(solution)/shard_map/first_chain/pallas_call | solution.py:271
  23.4 0.0 copy-done.4
  23.5 3.5 %all-to-all-start = ((f32[8,144,128]{2,1,0:T(8,128)}), f32[8,144,128]{2,1,0:T(8,128)S(1)}, u32[]{:S(2)}, u32[]{:S(2)}) async-start(f32[8,144,128]{2,1,0:T(8,128)} %get-tuple-element.20), calls=%async_computation | async-start | bytes 1179648 | tf_op jit(solution)/shard_map/all_to_all | solution.py:472
  27.0 1.9 %collective-permute-start.5 = (f32[32,4224]{1,0:T(8,128)S(1)}, f32[32,4224]{1,0:T(8,128)S(1)}, u32[]{:S(2)}, u32[]{:S(2)}) collective-permute-start(f32[32,4224]{1,0:T(8,128)S(1)} %get-tuple-element.19.value_ref), channel_id=1, source_target_pairs={{0,32},{32,64},{64,96},{96,128},{128,160},{160,192},{192,224},{224... | collective-permute-start | bytes 1622024 | tf_op jit(solution)/shard_map/ppermute | solution.py:473
  28.9 11.4 %all-to-all-done.parts_ref = f32[8,144,128]{2,1,0:T(8,128)S(1)} async-done(((f32[8,144,128]{2,1,0:T(8,128)}), f32[8,144,128]{2,1,0:T(8,128)S(1)}, u32[]{:S(2)}, u32[]{:S(2)}) %all-to-all-start) | async-done | bytes 589856 | tf_op jit(solution)/shard_map/all_to_all | solution.py:472
  40.3 6.6 %coarse_solve.1 = f32[8,128,128]{2,1,0:T(8,128)} custom-call(f32[8,144,128]{2,1,0:T(8,128)S(1)} %all-to-all-done.parts_ref, bf16[2,80,128]{2,1,0:T(8,128)(2,1)S(1)} %get-tuple-element.18.weights_ref), custom_call_target="tpu_custom_call" | custom-call | flops 8053063680 | bytes 1179648 | tf_op jit(solution)/shard_map/coarse_solve/pallas_call | solution.py:335
  46.9 3.5 %all-to-all-start.1 = ((f32[8,128,128]{2,1,0:T(8,128)}), f32[8,128,128]{2,1,0:T(8,128)S(1)}, u32[]{:S(2)}, u32[]{:S(2)}) async-start(f32[8,128,128]{2,1,0:T(8,128)} %coarse_solve.1), calls=%async_computation.1 | async-start | bytes 1048576 | tf_op jit(solution)/shard_map/all_to_all | solution.py:475
  50.4 1.5 %collective-permute-done.5.begin_ref = f32[32,4224]{1,0:T(8,128)S(1)} collective-permute-done((f32[32,4224]{1,0:T(8,128)S(1)}, f32[32,4224]{1,0:T(8,128)S(1)}, u32[]{:S(2)}, u32[]{:S(2)}) %collective-permute-start.5) | collective-permute-done | bytes 540704 | tf_op jit(solution)/shard_map/ppermute | solution.py:473
  51.9 0.0 copy-start.5
  51.9 2.2 %copy-done.5 = f32[8,32,4096]{2,1,0:T(8,128)S(1)} copy-done((f32[8,32,4096]{2,1,0:T(8,128)S(1)}, f32[8,32,4096]{2,1,0:T(8,128)}, u32[]{:S(2)}) %copy-start.5) | copy-done | bytes 4194328
  54.1 4.2 %second_chain.1.states_ref = f32[8,32,4096]{2,1,0:T(8,128)} custom-call(f32[8,32,4096]{2,1,0:T(8,128)S(1)} %copy-done.5, f32[32,4224]{1,0:T(8,128)S(1)} %collective-permute-done.5.begin_ref, f32[32,4096]{1,0:T(8,128)S(1)} %copy-done.1, f32[10,8,128]{2,1,0:T(8,128)S(1)} %collective-permute-done.1.left_ref, ...), custom_call_target="tpu_custom_call" | custom-call | flops 5368709120 | bytes 16777216 | tf_op jit(solution)/shard_map/second_chain/pallas_call | solution.py:405
  58.3 4.8 %all-to-all-done.1.parts_ref = f32[8,128,128]{2,1,0:T(8,128)S(1)} async-done(((f32[8,128,128]{2,1,0:T(8,128)}), f32[8,128,128]{2,1,0:T(8,128)S(1)}, u32[]{:S(2)}, u32[]{:S(2)}) %all-to-all-start.1) | async-done | bytes 524320 | tf_op jit(solution)/shard_map/all_to_all | solution.py:475
  63.1 0.8 %correct_last.1 = f32[8,32,4096]{2,1,0:T(8,128)} custom-call(f32[32,4224]{1,0:T(8,128)S(1)} %get-tuple-element.19.value_ref, f32[8,128,128]{2,1,0:T(8,128)S(1)} %all-to-all-done.1.parts_ref, f32[8,32,4096]{2,1,0:T(8,128)} %second_chain.1.states_ref), custom_call_target="tpu_custom_call", output_to_operand_aliasing={{}: (2, {})} | custom-call | tf_op jit(solution)/shard_map/correct_last/pallas_call | solution.py:436
Async XLA Ops:
  0.0 8.4 %copy-start.2 = (f32[4,16,16]{2,1,0:T(8,128)S(1)}, f32[4,16,16]{2,1,0:T(8,128)}, u32[]{:S(2)}) copy-start(f32[4,16,16]{2,1,0:T(8,128)} %fine_ref.1) | copy-start | bytes 12292
  0.0 8.4 %copy-start.3 = (f32[4,16,16]{2,1,0:T(8,128)S(1)}, f32[4,16,16]{2,1,0:T(8,128)}, u32[]{:S(2)}) copy-start(f32[4,16,16]{2,1,0:T(8,128)} %coarse_ref.1) | copy-start | bytes 12292
  0.0 18.6 %collective-permute-start = (f32[32,4096]{1,0:T(8,128)}, f32[32,4096]{1,0:T(8,128)S(1)}, u32[]{:S(2)}, u32[]{:S(2)}) collective-permute-start(f32[32,4096]{1,0:T(8,128)} %bitcast.1), channel_id=1, source_target_pairs={{0,32},{32,64},{64,96},{96,128},{128,160},{160,192},{192,224},{224... | collective-permute-start | bytes 1572872 | tf_op jit(solution)/shard_map/ppermute | solution.py:462
  3.3 15.3 %copy-start = (f32[1,32,4096]{2,1,0:T(8,128)S(1)}, f32[1,32,4096]{2,1,0:T(8,128)}, u32[]{:S(2)}) copy-start(f32[1,32,4096]{2,1,0:T(8,128)} %guess_ref.1) | copy-start | bytes 1572868
  3.3 15.3 %copy-start.1 = (f32[32,4096]{1,0:T(8,128)S(1)}, f32[32,4096]{1,0:T(8,128)}, u32[]{:S(2)}) copy-start(f32[32,4096]{1,0:T(8,128)} %initial_ref.3) | copy-start | bytes 1572868
  3.3 15.3 %collective-permute-start.1 = (f32[10,8,128]{2,1,0:T(8,128)}, f32[10,8,128]{2,1,0:T(8,128)S(1)}, u32[]{:S(2)}, u32[]{:S(2)}) collective-permute-start(f32[10,8,128]{2,1,0:T(8,128)} %get-tuple-element.14), channel_id=1, source_target_pairs={{0,1},{1,2},{2,3},{3,4},{4,5},{5,6},{6,7},{7,8},{8,9},{9,10},{10,1... | collective-permute-start | bytes 122888 | tf_op jit(solution)/shard_map/ppermute | solution.py:465
  3.4 15.2 %collective-permute-start.2 = (f32[10,8,128]{2,1,0:T(8,128)}, f32[10,8,128]{2,1,0:T(8,128)S(1)}, u32[]{:S(2)}, u32[]{:S(2)}) collective-permute-start(f32[10,8,128]{2,1,0:T(8,128)} %get-tuple-element.15), channel_id=1, source_target_pairs={{1,0},{2,1},{3,2},{4,3},{5,4},{6,5},{7,6},{8,7},{9,8},{10,9},{11,1... | collective-permute-start | bytes 122888 | tf_op jit(solution)/shard_map/ppermute | solution.py:464
  5.1 9.9 %collective-permute-start.3 = (f32[8,128]{1,0:T(8,128)}, f32[8,128]{1,0:T(8,128)S(1)}, u32[]{:S(2)}, u32[]{:S(2)}) collective-permute-start(f32[8,128]{1,0:T(8,128)} %get-tuple-element.16), channel_id=1, source_target_pairs={{0,33},{1,34},{2,35},{3,36},{4,37},{5,38},{6,39},{7,40},{8,41},{9,... | collective-permute-start | bytes 12296 | tf_op jit(solution)/shard_map/ppermute | solution.py:467
  7.6 9.5 %collective-permute-start.4 = (f32[8,128]{1,0:T(8,128)}, f32[8,128]{1,0:T(8,128)S(1)}, u32[]{:S(2)}, u32[]{:S(2)}) collective-permute-start(f32[8,128]{1,0:T(8,128)} %get-tuple-element.17), channel_id=1, source_target_pairs={{1,32},{2,33},{3,34},{4,35},{5,36},{6,37},{7,38},{8,39},{9,40},{10... | collective-permute-start | bytes 12296 | tf_op jit(solution)/shard_map/ppermute | solution.py:466
  10.6 12.8 %copy-start.4 = (f32[8,32,4096]{2,1,0:T(8,128)}, f32[8,32,4096]{2,1,0:T(8,128)S(1)}, u32[]{:S(2)}) copy-start(f32[8,32,4096]{2,1,0:T(8,128)S(1)} %get-tuple-element.13.forcing_ref) | copy-start | bytes 12582916
  23.5 16.9 %all-to-all-start = ((f32[8,144,128]{2,1,0:T(8,128)}), f32[8,144,128]{2,1,0:T(8,128)S(1)}, u32[]{:S(2)}, u32[]{:S(2)}) async-start(f32[8,144,128]{2,1,0:T(8,128)} %get-tuple-element.20), calls=%async_computation | async-start | bytes 1179648 | tf_op jit(solution)/shard_map/all_to_all | solution.py:472
  27.0 24.9 %collective-permute-start.5 = (f32[32,4224]{1,0:T(8,128)S(1)}, f32[32,4224]{1,0:T(8,128)S(1)}, u32[]{:S(2)}, u32[]{:S(2)}) collective-permute-start(f32[32,4224]{1,0:T(8,128)S(1)} %get-tuple-element.19.value_ref), channel_id=1, source_target_pairs={{0,32},{32,64},{64,96},{96,128},{128,160},{160,192},{192,224},{224... | collective-permute-start | bytes 1622024 | tf_op jit(solution)/shard_map/ppermute | solution.py:473
  46.9 16.2 %all-to-all-start.1 = ((f32[8,128,128]{2,1,0:T(8,128)}), f32[8,128,128]{2,1,0:T(8,128)S(1)}, u32[]{:S(2)}, u32[]{:S(2)}) async-start(f32[8,128,128]{2,1,0:T(8,128)} %coarse_solve.1), calls=%async_computation.1 | async-start | bytes 1048576 | tf_op jit(solution)/shard_map/all_to_all | solution.py:475
  51.9 2.2 %copy-start.5 = (f32[8,32,4096]{2,1,0:T(8,128)S(1)}, f32[8,32,4096]{2,1,0:T(8,128)}, u32[]{:S(2)}) copy-start(f32[8,32,4096]{2,1,0:T(8,128)} %copy-done.4) | copy-start | bytes 12582916

commit v2 on v1

v2 whole, which is shorter than its diff:
```python
import jax
import jax.numpy as jnp
from jax import lax
from jax.experimental import pallas as pl
from jax.experimental.pallas import tpu as pltpu
from jax.sharding import PartitionSpec as P

LANES = 128
REACH = 32
COND = 16
ROWS = 2 * COND
ONCE = 5 * COND
TWICE = 9 * COND
FINE, COARSE, COARSE_TWICE, OPERATORS = 0, ONCE, 2 * ONCE, 2 * ONCE + TWICE
VMEM_LIMIT = 20 * 1024 * 1024


def iota(shape, axis):
    return lax.broadcasted_iota(jnp.int32, shape, axis)


def pack_edge(tile, base):
    lane = iota((8, LANES), 1)
    out = jnp.zeros((8, LANES), jnp.float32)
    for g in range(4):
        part = pltpu.roll(tile[8 * g : 8 * g + 8], (REACH * g - base) % LANES, 1)
        out = jnp.where(lane // REACH == g, part, out)
    return out


def unpack_edge(packed, base):
    return jnp.concatenate(
        [pltpu.roll(packed, (base - REACH * g) % LANES, 1) for g in range(4)], axis=0
    )


def halo_of_edges(from_left, from_right):
    lane = iota((ROWS, LANES), 1)
    right = jnp.where(lane < REACH, unpack_edge(from_right, 0), 0.0)
    return jnp.where(lane >= LANES - REACH, unpack_edge(from_left, LANES - REACH), right)


def pack_halo(halo):
    lane = iota((COND, LANES), 1)
    outer = (lane < REACH) | (lane >= LANES - REACH)
    return jnp.where(outer, halo[:COND], pltpu.roll(halo[COND:], LANES // 2, 1))


def unpack_halo(packed):
    return jnp.concatenate([packed, pltpu.roll(packed, LANES // 2, 1)], axis=0)


def join_halo(right, left):
    return jnp.where(iota((ROWS, LANES), 1) < LANES // 2, right, left)


def mirror_halo(first, last):
    lane = iota((COND, LANES), 1)
    back = LANES - 1 - lane

    def pick(tile, index):
        return jnp.take_along_axis(tile, index, axis=1)

    left_v = pick(first[:COND], back)
    left_i = jnp.where(lane == LANES - 1, 0.0, -pick(first[COND:], jnp.maximum(back - 1, 0)))
    right_v = jnp.where(lane == 0, 0.0, -pick(last[:COND], jnp.minimum(back + 1, LANES - 1)))
    right_i = pick(last[COND:], back)
    return jnp.concatenate([left_v, left_i], axis=0), jnp.concatenate([right_v, right_i], axis=0)


def make_halo(from_left, from_right, first, last):
    space = lax.axis_index("space")
    left, right = mirror_halo(first, last)
    halo = halo_of_edges(from_left, from_right)
    is_right = iota((ROWS, LANES), 1) < LANES // 2
    halo = jnp.where(is_right & (space == lax.axis_size("space") - 1), right, halo)
    return jnp.where(jnp.logical_not(is_right) & (space == 0), left, halo)


def split(state):
    high = state.astype(jnp.bfloat16)
    low = (state - high.astype(jnp.float32)).astype(jnp.bfloat16)
    return jnp.concatenate([high, high, low, high], axis=0)


def lower(added, current):
    return jnp.concatenate([added[:COND], added[COND:] + current], axis=0)


def multiply(weights, state):
    return jnp.dot(weights, split(state), preferred_element_type=jnp.float32)


def step(state, weights, width):
    return shift_once(multiply(weights, state), width)


def shift_once(product, width):
    outs = []
    for b in range(0, product.shape[1], width):
        e = b + width
        out = product[:ROWS, b:e] + pltpu.roll(product[ROWS : 2 * ROWS, b:e], 1, 1)
        outs.append(lower(out, pltpu.roll(product[2 * ROWS :, b:e], width - 1, 1)))
    return outs[0] if len(outs) == 1 else jnp.concatenate(outs, axis=1)


def shift_twice(product, width):
    outs = []
    for b in range(0, product.shape[1], width):
        e = b + width
        out = product[:ROWS, b:e]
        for m, shift in ((1, 1), (2, width - 1), (3, 2)):
            out = out + pltpu.roll(product[m * ROWS : (m + 1) * ROWS, b:e], shift, 1)
        outs.append(lower(out, pltpu.roll(product[4 * ROWS :, b:e], width - 2, 1)))
    return outs[0] if len(outs) == 1 else jnp.concatenate(outs, axis=1)


def tile_of(ref, k):
    return ref[:, k * LANES : (k + 1) * LANES]


def step_tiles(load, store, count, weights, ring, group):
    first = iota((ROWS, LANES), 1) == 0
    last = iota((COND, LANES), 1) == LANES - 1
    here, before, after = {}, {}, {}
    order = [count - 1, *range(count - 1)] if ring else list(range(count))
    for at in range(0, count, group):
        some = order[at : at + group]
        product = multiply(weights, jnp.concatenate([load(k) for k in some], axis=1))
        for j, k in enumerate(some):
            part = product[:, j * LANES : (j + 1) * LANES]
            here[k] = part[:ROWS]
            before[k] = pltpu.roll(part[ROWS : 2 * ROWS], 1, 1)
            after[k] = pltpu.roll(part[2 * ROWS :], LANES - 1, 1)
        for k in list(here):
            left, right = k - 1, k + 1
            if ring:
                left, right = left % count, right % count
            elif k == 0:
                left = k
            elif k == count - 1:
                right = k
            if left in before and right in after:
                tile = here.pop(k) + jnp.where(first, before[left], before[k])
                store(k, lower(tile, jnp.where(last, after[right], after[k])))


def prepare_kernel(fine_ref, coarse_ref, forcing_ref, out_ref, staged_ref, sem):
    copy = pltpu.make_async_copy(forcing_ref, staged_ref, sem)
    copy.start()

    def product(a, b):
        return jnp.dot(
            a, b, precision=lax.Precision.HIGHEST, preferred_element_type=jnp.float32
        )

    def put(at, whole):
        high = whole.astype(jnp.bfloat16)
        rest = whole - high.astype(jnp.float32)
        low = rest.astype(jnp.bfloat16)
        least = (rest - low.astype(jnp.float32)).astype(jnp.bfloat16)
        parts = jnp.concatenate([high, low, high, least], axis=1)
        out_ref[at : at + whole.shape[0], :] = parts

    for m, blocks_ref in enumerate((fine_ref, coarse_ref)):
        p_v, k_v, p_i, k_i = (blocks_ref[r] for r in range(4))
        k_pk = product(k_i, jnp.concatenate([p_v, k_v], axis=1))
        kp, kk = k_pk[:, :COND], k_pk[:, COND:]
        zero = jnp.zeros_like(kk)

        def block(a, b, c, d):
            top = jnp.concatenate([a, b], axis=1)
            return jnp.concatenate([top, jnp.concatenate([c, d], axis=1)], axis=0)

        own = block(p_v, -k_v, kp, p_i - 2.0 * kk)
        before = block(zero, k_v, zero, kk)
        after = block(zero, zero, -kp, kk)
        put(FINE if m == 0 else COARSE, jnp.concatenate([own, before, after[COND:]], axis=0))
        if m == 1:
            square = product(
                jnp.concatenate([own, before, after], axis=0),
                jnp.concatenate([own, before, after], axis=1),
            )

            def pair(a, b):
                return square[a * ROWS : (a + 1) * ROWS, b * ROWS : (b + 1) * ROWS]

            twice = [
                pair(0, 0) + pair(1, 2) + pair(2, 1),
                pair(0, 1) + pair(1, 0),
                pair(0, 2) + pair(2, 0),
                pair(1, 1),
                pair(2, 2)[COND:],
            ]
            put(COARSE_TWICE, jnp.concatenate(twice, axis=0))
    copy.wait()


def prepare(fine_blocks, coarse_blocks, forcing):
    vmem = pl.BlockSpec(memory_space=pltpu.VMEM)
    return pl.pallas_call(
        prepare_kernel,
        out_shape=(
            pltpu.VMEM((OPERATORS, 4 * ROWS), jnp.bfloat16),
            pltpu.VMEM(forcing.shape, jnp.float32),
        ),
        in_specs=[vmem, vmem, pl.BlockSpec(memory_space=pltpu.HBM)],
        out_specs=(vmem, vmem),
        scratch_shapes=[pltpu.SemaphoreType.DMA],
        compiler_params=pltpu.CompilerParams(vmem_limit_bytes=VMEM_LIMIT),
        name="prepare",
    )(fine_blocks, coarse_blocks, pltpu.with_memory_space_constraint(forcing, pltpu.HBM))


def edges_kernel(
    f_first, f_last, c_first, c_last, i_first, i_last, low_ref, high_ref, low_guess_ref, high_guess_ref
):
    count = f_first.shape[0]
    for n in range(count):
        low_ref[n] = pack_edge(f_first[n], 0)
        high_ref[n] = pack_edge(f_last[n], LANES - REACH)
    low_guess_ref[...] = pack_edge(c_first[0], 0)
    high_guess_ref[...] = pack_edge(c_last[0], LANES - REACH)
    low_ref[count] = low_guess_ref[...]
    high_ref[count] = high_guess_ref[...]
    low_ref[count + 1] = pack_edge(i_first[...], 0)
    high_ref[count + 1] = pack_edge(i_last[...], LANES - REACH)


def cut_edges(forcing, c_guess, initial):
    count, _, length = forcing.shape
    end = length // LANES - 1

    def both(shape, at):
        return [pl.BlockSpec(shape, lambda g, a=a: at(a)) for a in (0, end)]

    shape = jax.ShapeDtypeStruct((count + 2, 8, LANES), jnp.float32)
    whole = pl.BlockSpec(shape.shape, lambda g: (0, 0, 0))
    guess = jax.ShapeDtypeStruct((8, LANES), jnp.float32)
    whole_guess = pl.BlockSpec(guess.shape, lambda g: (0, 0))
    return pl.pallas_call(
        edges_kernel,
        grid=(1,),
        out_shape=(shape, shape, guess, guess),
        in_specs=both((count, ROWS, LANES), lambda a: (0, 0, a))
        + both((1, ROWS, LANES), lambda a: (0, 0, a))
        + both((ROWS, LANES), lambda a: (0, a)),
        out_specs=(whole, whole, whole_guess, whole_guess),
        name="edges",
    )(forcing, forcing, c_guess, c_guess, initial, initial)


def write_parts(out_ref, main, halo, at):
    groups = out_ref.shape[0]
    length = main.shape[1]
    part = length // groups
    tiles = part // LANES

    def tile(k):
        if k < 0 or k == length // LANES:
            return halo
        return main[:, k * LANES : (k + 1) * LANES]

    for j in range(groups):
        for i in range(tiles):
            out_ref[j, at + ROWS * i : at + ROWS * (i + 1), :] = tile(j * tiles + i)
        rim = join_halo(tile((j + 1) * tiles), tile(j * tiles - 1))
        out_ref[j, at + ROWS * tiles : at + ROWS * tiles + COND, :] = pack_halo(rim)


def source_halo_kernel(forcing_ref, left_ref, right_ref, halo_ref):
    count, _, length = forcing_ref.shape
    for n in range(count):
        halo_ref[n] = make_halo(
            left_ref[n], right_ref[n], forcing_ref[n, :, :LANES], forcing_ref[n, :, length - LANES :]
        )


def source_halos(forcing, left, right):
    vmem = pl.BlockSpec(memory_space=pltpu.VMEM)
    return pl.pallas_call(
        source_halo_kernel,
        out_shape=pltpu.VMEM((forcing.shape[0], ROWS, LANES), jnp.float32),
        in_specs=[vmem] * 3,
        out_specs=vmem,
        compiler_params=pltpu.CompilerParams(vmem_limit_bytes=VMEM_LIMIT),
        name="source_halos",
    )(forcing, left, right)


def start_chain(main_ref, begin_ref, initial_ref, sem):
    is_first = lax.axis_index("tm") == 0

    @pl.when(is_first)
    def _():
        pltpu.make_async_copy(initial_ref, main_ref, sem).start()

    @pl.when(jnp.logical_not(is_first))
    def _():
        pltpu.make_async_copy(begin_ref, main_ref, sem).start()

    return pltpu.make_async_copy(begin_ref, main_ref, sem)


def halo_of(main_ref, from_left, from_right):
    length = main_ref.shape[1]
    return make_halo(from_left, from_right, main_ref[:, :LANES], main_ref[:, length - LANES :])


def first_kernel(
    forcing_ref,
    source_halo_ref,
    begin_ref,
    initial_ref,
    guess_ref,
    left_ref,
    right_ref,
    begin_left_ref,
    begin_right_ref,
    weights_ref,
    out_ref,
    value_ref,
    own_ref,
    even_ref,
    odd_ref,
    sem,
):
    steps, _, length = forcing_ref.shape
    tiles = length // LANES
    guess_at, initial_at = left_ref.shape[0] - 2, left_ref.shape[0] - 1
    own = pltpu.make_async_copy(guess_ref.at[0], own_ref, sem)
    own.start()
    is_first = lax.axis_index("tm") == 0

    def begin(k):
        return jnp.where(is_first, tile_of(initial_ref, k), tile_of(begin_ref, k))

    begin_halo = make_halo(
        jnp.where(is_first, left_ref[initial_at], begin_left_ref[...]),
        jnp.where(is_first, right_ref[initial_at], begin_right_ref[...]),
        begin(0),
        begin(tiles - 1),
    )
    states = (even_ref, odd_ref)
    for n in range(steps):

        def load(k, n=n):
            if n > 0:
                return tile_of(states[n % 2], k)
            return begin(k - 1) if 0 < k <= tiles else begin_halo

        def store(k, tile, n=n):
            inside = 0 < k <= tiles
            tile = tile + (tile_of(forcing_ref.at[n], k - 1) if inside else source_halo_ref[n])
            if n == steps - 1 and inside:
                value_ref[:, (k - 1) * LANES : k * LANES] = tile
            else:
                states[(n + 1) % 2][:, k * LANES : (k + 1) * LANES] = tile

        step_tiles(load, store, tiles + 2, weights_ref[FINE:COARSE], False, 2)

    end = states[steps % 2]
    halo = join_halo(tile_of(end, tiles + 1), tile_of(end, 0))
    value_ref[:, length:] = halo
    own.wait()
    guess_halo = make_halo(
        left_ref[guess_at], right_ref[guess_at], tile_of(own_ref, 0), tile_of(own_ref, tiles - 1)
    )
    write_parts(out_ref, value_ref[:, :length] - own_ref[...], halo - guess_halo, 0)


def first_chain(
    forcing,
    source_halo,
    begin,
    initial,
    c_guess,
    left,
    right,
    begin_left,
    begin_right,
    weights,
    groups,
):
    steps, _, length = forcing.shape
    rows = length // groups // LANES * ROWS + COND
    anywhere = pl.BlockSpec(memory_space=pl.ANY)
    vmem = pl.BlockSpec(memory_space=pltpu.VMEM)
    return pl.pallas_call(
        first_kernel,
        out_shape=(
            pltpu.VMEM((groups, rows, LANES), jnp.float32),
            pltpu.VMEM((ROWS, length + LANES), jnp.float32),
        ),
        in_specs=[vmem, vmem, vmem, vmem, anywhere, vmem, vmem, vmem, vmem, vmem],
        out_specs=(vmem, vmem),
        scratch_shapes=[
            pltpu.VMEM((ROWS, length), jnp.float32),
            pltpu.VMEM((ROWS, length + 2 * LANES), jnp.float32),
            pltpu.VMEM((ROWS, length + 2 * LANES), jnp.float32),
            pltpu.SemaphoreType.DMA,
        ],
        compiler_params=pltpu.CompilerParams(vmem_limit_bytes=VMEM_LIMIT),
        cost_estimate=cost(steps, length, forcing.size),
        name="first_chain",
    )(
        forcing,
        source_halo,
        begin,
        initial,
        c_guess,
        left,
        right,
        begin_left,
        begin_right,
        weights,
    )


def cost(steps, columns, elements):
    return pl.CostEstimate(
        flops=steps * columns * 80 * 128 * 16, bytes_accessed=8 * elements, transcendentals=0
    )


def coarse_kernel(parts_ref, weights_ref, out_ref, even_ref, odd_ref):
    groups = parts_ref.shape[0]
    tiles = (parts_ref.shape[1] - COND) // ROWS
    width = (tiles + 1) * LANES

    states = (even_ref, odd_ref)
    for n in range(8):
        for t in range(groups - 1):

            def load(k, n=n, t=t):
                if n > 0:
                    return tile_of(states[n % 2], t * (tiles + 1) + k)
                if k < tiles:
                    return parts_ref[t, ROWS * k : ROWS * (k + 1), :]
                return unpack_halo(parts_ref[t, ROWS * tiles : ROWS * tiles + COND, :])

            def store(k, tile, n=n, t=t):
                at = t * width + k * LANES
                states[(n + 1) % 2][:, at : at + LANES] = tile

            step_tiles(load, store, tiles + 1, weights_ref[FINE:COARSE], True, tiles + 1)

    def put(t, ring):
        for i in range(tiles):
            out_ref[t, ROWS * i : ROWS * (i + 1), :] = ring[:, i * LANES : (i + 1) * LANES]

    resid = [even_ref[:, t * width : (t + 1) * width] for t in range(groups - 1)]
    second = range(1, groups - 2, 2)
    carried = step(
        jnp.concatenate([resid[t] for t in second], axis=1),
        weights_ref[COARSE:COARSE_TWICE],
        width,
    )
    out_ref[0] = jnp.zeros_like(out_ref[0])
    correction = resid[0]
    put(1, correction)
    for m, t in enumerate(second):
        both = multiply(weights_ref[COARSE:OPERATORS], correction)
        put(t + 1, shift_once(both[:ONCE], width) + resid[t])
        together = carried[:, m * width : (m + 1) * width] + resid[t + 1]
        correction = shift_twice(both[ONCE:], width) + together
        put(t + 2, correction)


def coarse_solve(parts, weights):
    groups, rows, _ = parts.shape
    tiles = (rows - COND) // ROWS
    return pl.pallas_call(
        coarse_kernel,
        out_shape=pltpu.VMEM((groups, ROWS * tiles, LANES), jnp.float32),
        scratch_shapes=[pltpu.VMEM((ROWS, (groups - 1) * (tiles + 1) * LANES), jnp.float32)] * 2,
        compiler_params=pltpu.CompilerParams(vmem_limit_bytes=VMEM_LIMIT),
        cost_estimate=cost(12, groups * tiles * LANES, parts.size),
        name="coarse_solve",
    )(parts, weights)


def second_kernel(
    forcing_ref,
    source_halo_ref,
    begin_ref,
    initial_ref,
    left_ref,
    right_ref,
    weights_ref,
    out_ref,
    states_ref,
    halo_ref,
    sems,
    out_sems,
):
    steps = out_sems.shape[0]
    length = forcing_ref.shape[2]
    initial_at = left_ref.shape[0] - 1
    halo = pltpu.make_async_copy(begin_ref.at[:, length:], halo_ref, sems.at[1])
    halo.start()
    begun = start_chain(states_ref.at[0], begin_ref.at[:, :length], initial_ref, sems.at[0])
    halo.wait()
    begun.wait()

    @pl.when(lax.axis_index("tm") == 0)
    def _():
        halo_ref[...] = halo_of(states_ref.at[0], left_ref[initial_at], right_ref[initial_at])

    def result(n):
        return pltpu.make_async_copy(states_ref.at[n + 1], out_ref.at[n], out_sems.at[n])

    def one(n, carry):
        state = jnp.concatenate([states_ref[n], halo_ref[...]], axis=1)
        state = step(state, weights_ref[FINE:COARSE], length + LANES)
        states_ref[n + 1] = state[:, :length] + forcing_ref[n]
        halo_ref[...] = state[:, length:] + source_halo_ref[n]
        result(n).start()
        return carry

    lax.fori_loop(0, steps, one, 0)
    for n in range(steps):
        result(n).wait()


def second_chain(forcing, source_halo, begin, initial, left, right, weights):
    count, _, length = forcing.shape
    hbm = pl.BlockSpec(memory_space=pltpu.HBM)
    anywhere = pl.BlockSpec(memory_space=pl.ANY)
    vmem = pl.BlockSpec(memory_space=pltpu.VMEM)
    return pl.pallas_call(
        second_kernel,
        out_shape=jax.ShapeDtypeStruct(forcing.shape, jnp.float32),
        in_specs=[vmem, vmem, anywhere, anywhere, vmem, vmem, vmem],
        out_specs=hbm,
        scratch_shapes=[
            pltpu.VMEM(forcing.shape, jnp.float32),
            pltpu.VMEM((ROWS, LANES), jnp.float32),
            pltpu.SemaphoreType.DMA((2,)),
            pltpu.SemaphoreType.DMA((count - 1,)),
        ],
        compiler_params=pltpu.CompilerParams(vmem_limit_bytes=VMEM_LIMIT),
        cost_estimate=cost(count, length, 2 * forcing.size),
        name="second_chain",
    )(forcing, source_halo, begin, initial, left, right, weights)


def correct_kernel(value_ref, parts_ref, states_ref, out_ref):
    del states_ref
    groups = parts_ref.shape[0]
    tiles = out_ref.shape[2] // groups // LANES
    for j in range(groups):
        for i in range(tiles):
            at = (j * tiles + i) * LANES
            out_ref[0, :, at : at + LANES] = (
                value_ref[:, at : at + LANES] + parts_ref[j, ROWS * i : ROWS * (i + 1), :]
            )


def correct_last(value, parts, states):
    count, _, length = states.shape
    return pl.pallas_call(
        correct_kernel,
        grid=(1,),
        out_shape=jax.ShapeDtypeStruct(states.shape, jnp.float32),
        in_specs=[
            pl.BlockSpec(value.shape, lambda g: (0, 0)),
            pl.BlockSpec(parts.shape, lambda g: (0, 0, 0)),
            pl.BlockSpec(memory_space=pl.ANY),
        ],
        out_specs=pl.BlockSpec((1, ROWS, length), lambda g: (count - 1, 0, 0)),
        input_output_aliases={2: 0},
        compiler_params=pltpu.CompilerParams(vmem_limit_bytes=VMEM_LIMIT),
        name="correct_last",
    )(value, parts, states)


def body(initial, c_guess, forcing, fine_blocks, coarse_blocks):
    groups = lax.axis_size("tm")
    spaces = lax.axis_size("space")
    up = [(i, (i + 1) % spaces) for i in range(spaces)]
    down = [(b, a) for a, b in up]
    to_next = [(i, (i + 1) % groups) for i in range(groups)]

    def to_next_and(pairs):
        return [(t * spaces + a, u * spaces + b) for t, u in to_next for a, b in pairs]

    begin = lax.ppermute(c_guess[0], "tm", to_next)
    low, high, low_guess, high_guess = cut_edges(forcing, c_guess, initial)
    right = lax.ppermute(low, "space", down)
    left = lax.ppermute(high, "space", up)
    begin_right = lax.ppermute(low_guess, ("tm", "space"), to_next_and(down))
    begin_left = lax.ppermute(high_guess, ("tm", "space"), to_next_and(up))
    weights, staged = prepare(fine_blocks, coarse_blocks, forcing)
    source_halo = source_halos(staged, left, right)
    parts, value = first_chain(
        staged,
        source_halo,
        begin,
        initial,
        c_guess,
        left,
        right,
        begin_left,
        begin_right,
        weights,
        groups,
    )
    parts = lax.all_to_all(parts, "tm", 0, 0, tiled=True)
    begin = lax.ppermute(value, "tm", to_next)
    parts = coarse_solve(parts, weights)
    parts = lax.all_to_all(parts, "tm", 0, 0, tiled=True)
    states = second_chain(staged, source_halo, begin, initial, left, right, weights)
    return correct_last(value, parts, states)


def solution(mesh):
    in_specs = (P(None, "space"), P("tm", None, "space"), P("tm", None, "space"), P(), P())
    out_specs = P("tm", None, "space")
    return jax.shard_map(body, mesh=mesh, in_specs=in_specs, out_specs=out_specs, check_vma=False)
```

time: 64.3 us -> 60.5 us (0.941)
  Pallas kernels: 20.4 us -> 17.5 us
  waiting for transfers between devices: 25.7 us -> 24.8 us
    ppermute x1, waiting for transfers between devices: 1.52 us -> 7.28 us  [body(): left = lax.ppermute(high, 'space', up)]
    ppermute x1, waiting for transfers between devices: 4.36 us -> 0.01 us  [body(): begin_left = lax.ppermute(high_guess, ('tm', 'space'), to_next_and(up))]
    pallas_call x3 -> x4, Pallas kernels: 13.6 us -> 10.7 us  [the longest x1 4.07 us: coarse_solve(): pl.pallas_call(coarse_kernel, out_shape=pltpu.VMEM((groups, ROWS * tiles,...]
    all_to_all x2, waiting for transfers between devices: 16.2 us -> 13.5 us  [body(): parts = lax.all_to_all(parts, 'tm', 0, 0, tiled=True)]
    ppermute x1, waiting for transfers between devices: 1.5 us -> 4.02 us  [body(): begin = lax.ppermute(value, 'tm', to_next)]
    ppermute x1, waiting for transfers between devices: 2.06 us -> 0.01 us  [body(): begin_right = lax.ppermute(low_guess, ('tm', 'space'), to_next_and(down))]
  transfers between devices with their start and end apart: 8 -> 8, of which waited for: 6 -> 4; matrix products, arithmetic and copies ran while one was open for 0% -> 0% of each run, Pallas kernels for 23% -> 22%
where the time goes in v2:
time: 60.5 us; the launch traced here: 60.2 us
  waiting for transfers between devices  24.8 us (41%)
  Pallas kernels  17.5 us (29%)
  starting transfers between devices  15.5 us (26%)
  local copies, waits for them, and re-layouts  2.21 us (4%)
    all_to_all x2, waiting for transfers between devices, body(): parts = lax.all_to_all(parts, 'tm', 0, 0, tiled=True)  13.5 us
    ppermute x1, waiting for transfers between devices, body(): left = lax.ppermute(high, 'space', up)  7.28 us
    all_to_all x2, starting transfers between devices, body(): parts = lax.all_to_all(parts, 'tm', 0, 0, tiled=True)  7.04 us
    pallas_call x1, Pallas kernels, second_chain(): pl.pallas_call(second_kernel, out_shape=jax.ShapeDtypeStruct(forcing.shap...  4.18 us
    pallas_call x1, Pallas kernels, coarse_solve(): pl.pallas_call(coarse_kernel, out_shape=pltpu.VMEM((groups, ROWS * tiles,...  4.07 us
    ppermute x1, waiting for transfers between devices, body(): begin = lax.ppermute(value, 'tm', to_next)  4.02 us
    pallas_call x1, Pallas kernels, first_chain(): pl.pallas_call(first_kernel, out_shape=(pltpu.VMEM((groups, rows, LANES),...  3.49 us
    pallas_call x1, Pallas kernels, prepare(): pl.pallas_call(prepare_kernel, out_shape=(pltpu.VMEM((OPERATORS, 4 * ROWS...  2.94 us
  transfers between devices with their start and end apart: 8, of which 4 were waited for; matrix products, arithmetic and copies ran while one was open for 0% of the time, Pallas kernels for 22%

profile of v2, /device:TPU:104, one launch (start us, length us, event | category | flops | bytes accessed | tf_op | source)
XLA Modules:
  0.0 60.2 jit_solution(3341492969950109474)
XLA Ops:
  0.0 0.0 copy-start.4
  0.0 0.0 copy-start.5
  0.0 1.5 %collective-permute-start.2 = (f32[32,4096]{1,0:T(8,128)}, f32[32,4096]{1,0:T(8,128)S(1)}, u32[]{:S(2)}, u32[]{:S(2)}) collective-permute-start(f32[32,4096]{1,0:T(8,128)} %bitcast.1), channel_id=1, source_target_pairs={{0,32},{32,64},{64,96},{96,128},{128,160},{160,192},{192,224},{224... | collective-permute-start | bytes 1572872 | tf_op jit(solution)/shard_map/ppermute | solution.py:588
  1.5 1.8 %edges.1 = (f32[10,8,128]{2,1,0:T(8,128)}, f32[10,8,128]{2,1,0:T(8,128)}, f32[8,128]{1,0:T(8,128)}, f32[8,128]{1,0:T(8,128)}) custom-call(f32[8,32,4096]{2,1,0:T(8,128)} %f_last.1, f32[8,32,4096]{2,1,0:T(8,128)} %f_last.1, f32[1,32,4096]{2,1,0:T(8,128)} %guess_ref.1, f32[1,32,4096]{2,1,0:T(8,128)} %guess_ref.1, f32[32,4096]{1,0:T(8,128)} %initial_ref.3, ...), custom_call_target="tpu_custom_call" | custom-call | tf_op jit(solution)/shard_map/edges/pallas_call | solution.py:241
  3.3 0.0 collective-permute-start
  3.3 1.7 %collective-permute-start.1 = (f32[10,8,128]{2,1,0:T(8,128)}, f32[10,8,128]{2,1,0:T(8,128)S(1)}, u32[]{:S(2)}, u32[]{:S(2)}) collective-permute-start(f32[10,8,128]{2,1,0:T(8,128)} %get-tuple-element.15), channel_id=1, source_target_pairs={{1,0},{2,1},{3,2},{4,3},{5,4},{6,5},{7,6},{8,7},{9,8},{10,9},{11,1... | collective-permute-start | bytes 122888 | tf_op jit(solution)/shard_map/ppermute | solution.py:590
  5.0 2.5 %collective-permute-start.3 = (f32[8,128]{1,0:T(8,128)}, f32[8,128]{1,0:T(8,128)S(1)}, u32[]{:S(2)}, u32[]{:S(2)}) collective-permute-start(f32[8,128]{1,0:T(8,128)} %get-tuple-element.16), channel_id=1, source_target_pairs={{0,33},{1,34},{2,35},{3,36},{4,37},{5,38},{6,39},{7,40},{8,41},{9,... | collective-permute-start | bytes 12296 | tf_op jit(solution)/shard_map/ppermute | solution.py:593
  7.5 0.0 copy-start.2
  7.5 0.0 copy-start.3
  7.5 0.8 %collective-permute-start.4 = (f32[8,128]{1,0:T(8,128)}, f32[8,128]{1,0:T(8,128)S(1)}, u32[]{:S(2)}, u32[]{:S(2)}) collective-permute-start(f32[8,128]{1,0:T(8,128)} %get-tuple-element.17), channel_id=1, source_target_pairs={{1,32},{2,33},{3,34},{4,35},{5,36},{6,37},{7,38},{8,39},{9,40},{10... | collective-permute-start | bytes 12296 | tf_op jit(solution)/shard_map/ppermute | solution.py:592
  8.3 0.0 copy-done.4
  8.3 0.0 copy-done.5
  8.3 2.9 %prepare.1 = (bf16[304,128]{1,0:T(8,128)(2,1)S(1)}, f32[8,32,4096]{2,1,0:T(8,128)S(1)}) custom-call(f32[4,16,16]{2,1,0:T(8,128)S(1)} %copy-done.4, f32[4,16,16]{2,1,0:T(8,128)S(1)} %copy-done.5, f32[8,32,4096]{2,1,0:T(8,128)} %f_last.1), custom_call_target="tpu_custom_call" | custom-call | tf_op jit(solution)/shard_map/prepare/pallas_call | solution.py:201
  11.3 0.0 copy-start
  11.3 7.3 %collective-permute-done.left_ref = f32[10,8,128]{2,1,0:T(8,128)S(1)} collective-permute-done((f32[10,8,128]{2,1,0:T(8,128)}, f32[10,8,128]{2,1,0:T(8,128)S(1)}, u32[]{:S(2)}, u32[]{:S(2)}) %collective-permute-start) | collective-permute-done | bytes 40992 | tf_op jit(solution)/shard_map/ppermute | solution.py:591
  18.6 0.0 collective-permute-done.1.right_ref
  18.6 0.2 source_halos.1.source_halo_ref
  18.8 0.0 collective-permute-done.3.begin_left_ref
  18.8 0.0 collective-permute-done.4.begin_right_ref
  18.9 0.0 collective-permute-done.2.begin_ref
  18.9 0.0 copy-done.2
  18.9 0.0 copy-done.3
  18.9 3.5 %first_chain.1 = (f32[8,144,128]{2,1,0:T(8,128)}, f32[32,4224]{1,0:T(8,128)S(1)}) custom-call(f32[8,32,4096]{2,1,0:T(8,128)S(1)} %get-tuple-element.13.forcing_ref, f32[8,32,128]{2,1,0:T(8,128)S(1)} %source_halos.1.source_halo_ref, f32[32,4096]{1,0:T(8,128)S(1)} %collective-permute-done.2.begin_ref, f32[32,4096]{1,0:T(8,128)S(1)} %copy-done.3, ...), custom_call_target="tpu_custom_call" | custom-call | flops 5368709120 | bytes 8388608 | tf_op jit(solution)/shard_map/first_chain/pallas_call | solution.py:389
  22.4 0.0 copy-done
  22.4 3.5 %all-to-all-start = ((f32[8,144,128]{2,1,0:T(8,128)}), f32[8,144,128]{2,1,0:T(8,128)S(1)}, u32[]{:S(2)}, u32[]{:S(2)}) async-start(f32[8,144,128]{2,1,0:T(8,128)} %get-tuple-element.20), calls=%async_computation | async-start | bytes 1179648 | tf_op jit(solution)/shard_map/all_to_all | solution.py:609
  25.9 1.9 %collective-permute-start.5 = (f32[32,4224]{1,0:T(8,128)S(1)}, f32[32,4224]{1,0:T(8,128)S(1)}, u32[]{:S(2)}, u32[]{:S(2)}) collective-permute-start(f32[32,4224]{1,0:T(8,128)S(1)} %get-tuple-element.19.value_ref), channel_id=1, source_target_pairs={{0,32},{32,64},{64,96},{96,128},{128,160},{160,192},{192,224},{224... | collective-permute-start | bytes 1622024 | tf_op jit(solution)/shard_map/ppermute | solution.py:610
  27.9 11.6 %all-to-all-done.parts_ref = f32[8,144,128]{2,1,0:T(8,128)S(1)} async-done(((f32[8,144,128]{2,1,0:T(8,128)}), f32[8,144,128]{2,1,0:T(8,128)S(1)}, u32[]{:S(2)}, u32[]{:S(2)}) %all-to-all-start) | async-done | bytes 589856 | tf_op jit(solution)/shard_map/all_to_all | solution.py:609
  39.5 4.1 %coarse_solve.1 = f32[8,128,128]{2,1,0:T(8,128)} custom-call(f32[8,144,128]{2,1,0:T(8,128)S(1)} %all-to-all-done.parts_ref, bf16[304,128]{1,0:T(8,128)(2,1)S(1)} %get-tuple-element.18.weights_ref), custom_call_target="tpu_custom_call" | custom-call | flops 8053063680 | bytes 1179648 | tf_op jit(solution)/shard_map/coarse_solve/pallas_call | solution.py:473
  43.6 3.5 %all-to-all-start.1 = ((f32[8,128,128]{2,1,0:T(8,128)}), f32[8,128,128]{2,1,0:T(8,128)S(1)}, u32[]{:S(2)}, u32[]{:S(2)}) async-start(f32[8,128,128]{2,1,0:T(8,128)} %coarse_solve.1), calls=%async_computation.1 | async-start | bytes 1048576 | tf_op jit(solution)/shard_map/all_to_all | solution.py:612
  47.1 4.0 %collective-permute-done.5.begin_ref = f32[32,4224]{1,0:T(8,128)S(1)} collective-permute-done((f32[32,4224]{1,0:T(8,128)S(1)}, f32[32,4224]{1,0:T(8,128)S(1)}, u32[]{:S(2)}, u32[]{:S(2)}) %collective-permute-start.5) | collective-permute-done | bytes 540704 | tf_op jit(solution)/shard_map/ppermute | solution.py:610
  51.1 0.0 copy-start.1
  51.1 2.2 %copy-done.1 = f32[8,32,4096]{2,1,0:T(8,128)S(1)} copy-done((f32[8,32,4096]{2,1,0:T(8,128)S(1)}, f32[8,32,4096]{2,1,0:T(8,128)}, u32[]{:S(2)}) %copy-start.1) | copy-done | bytes 4194328
  53.3 4.2 %second_chain.1.states_ref = f32[8,32,4096]{2,1,0:T(8,128)} custom-call(f32[8,32,4096]{2,1,0:T(8,128)S(1)} %copy-done.1, f32[8,32,128]{2,1,0:T(8,128)S(1)} %source_halos.1.source_halo_ref, f32[32,4224]{1,0:T(8,128)S(1)} %collective-permute-done.5.begin_ref, f32[32,4096]{1,0:T(8,128)S(1)} %copy-done.3, f32[10,8,128]{2,1,0:T(8,128)S(1)} %collective-permute-done.left_ref, ...), custom_call_target="tpu_custom_call" | custom-call | flops 5368709120 | bytes 16777216 | tf_op jit(solution)/shard_map/second_chain/pallas_call | solution.py:531
  57.4 1.9 %all-to-all-done.1.parts_ref = f32[8,128,128]{2,1,0:T(8,128)S(1)} async-done(((f32[8,128,128]{2,1,0:T(8,128)}), f32[8,128,128]{2,1,0:T(8,128)S(1)}, u32[]{:S(2)}, u32[]{:S(2)}) %all-to-all-start.1) | async-done | bytes 524320 | tf_op jit(solution)/shard_map/all_to_all | solution.py:612
  59.3 0.8 %correct_last.1 = f32[8,32,4096]{2,1,0:T(8,128)} custom-call(f32[32,4224]{1,0:T(8,128)S(1)} %get-tuple-element.19.value_ref, f32[8,128,128]{2,1,0:T(8,128)S(1)} %all-to-all-done.1.parts_ref, f32[8,32,4096]{2,1,0:T(8,128)} %second_chain.1.states_ref), custom_call_target="tpu_custom_call", output_to_operand_aliasing={{}: (2, {})} | custom-call | tf_op jit(solution)/shard_map/correct_last/pallas_call | solution.py:562
Async XLA Ops:
  0.0 8.3 %copy-start.4 = (f32[4,16,16]{2,1,0:T(8,128)S(1)}, f32[4,16,16]{2,1,0:T(8,128)}, u32[]{:S(2)}) copy-start(f32[4,16,16]{2,1,0:T(8,128)} %fine_ref.1) | copy-start | bytes 12292
  0.0 8.3 %copy-start.5 = (f32[4,16,16]{2,1,0:T(8,128)S(1)}, f32[4,16,16]{2,1,0:T(8,128)}, u32[]{:S(2)}) copy-start(f32[4,16,16]{2,1,0:T(8,128)} %coarse_ref.1) | copy-start | bytes 12292
  0.0 18.9 %collective-permute-start.2 = (f32[32,4096]{1,0:T(8,128)}, f32[32,4096]{1,0:T(8,128)S(1)}, u32[]{:S(2)}, u32[]{:S(2)}) collective-permute-start(f32[32,4096]{1,0:T(8,128)} %bitcast.1), channel_id=1, source_target_pairs={{0,32},{32,64},{64,96},{96,128},{128,160},{160,192},{192,224},{224... | collective-permute-start | bytes 1572872 | tf_op jit(solution)/shard_map/ppermute | solution.py:588
  3.3 15.3 %collective-permute-start = (f32[10,8,128]{2,1,0:T(8,128)}, f32[10,8,128]{2,1,0:T(8,128)S(1)}, u32[]{:S(2)}, u32[]{:S(2)}) collective-permute-start(f32[10,8,128]{2,1,0:T(8,128)} %get-tuple-element.14), channel_id=1, source_target_pairs={{0,1},{1,2},{2,3},{3,4},{4,5},{5,6},{6,7},{7,8},{8,9},{9,10},{10,1... | collective-permute-start | bytes 122888 | tf_op jit(solution)/shard_map/ppermute | solution.py:591
  3.3 15.3 %collective-permute-start.1 = (f32[10,8,128]{2,1,0:T(8,128)}, f32[10,8,128]{2,1,0:T(8,128)S(1)}, u32[]{:S(2)}, u32[]{:S(2)}) collective-permute-start(f32[10,8,128]{2,1,0:T(8,128)} %get-tuple-element.15), channel_id=1, source_target_pairs={{1,0},{2,1},{3,2},{4,3},{5,4},{6,5},{7,6},{8,7},{9,8},{10,9},{11,1... | collective-permute-start | bytes 122888 | tf_op jit(solution)/shard_map/ppermute | solution.py:590
  5.0 13.8 %collective-permute-start.3 = (f32[8,128]{1,0:T(8,128)}, f32[8,128]{1,0:T(8,128)S(1)}, u32[]{:S(2)}, u32[]{:S(2)}) collective-permute-start(f32[8,128]{1,0:T(8,128)} %get-tuple-element.16), channel_id=1, source_target_pairs={{0,33},{1,34},{2,35},{3,36},{4,37},{5,38},{6,39},{7,40},{8,41},{9,... | collective-permute-start | bytes 12296 | tf_op jit(solution)/shard_map/ppermute | solution.py:593
  7.5 11.4 %copy-start.2 = (f32[1,32,4096]{2,1,0:T(8,128)S(1)}, f32[1,32,4096]{2,1,0:T(8,128)}, u32[]{:S(2)}) copy-start(f32[1,32,4096]{2,1,0:T(8,128)} %guess_ref.1) | copy-start | bytes 1572868
  7.5 11.4 %copy-start.3 = (f32[32,4096]{1,0:T(8,128)S(1)}, f32[32,4096]{1,0:T(8,128)}, u32[]{:S(2)}) copy-start(f32[32,4096]{1,0:T(8,128)} %initial_ref.3) | copy-start | bytes 1572868
  7.5 11.4 %collective-permute-start.4 = (f32[8,128]{1,0:T(8,128)}, f32[8,128]{1,0:T(8,128)S(1)}, u32[]{:S(2)}, u32[]{:S(2)}) collective-permute-start(f32[8,128]{1,0:T(8,128)} %get-tuple-element.17), channel_id=1, source_target_pairs={{1,32},{2,33},{3,34},{4,35},{5,36},{6,37},{7,38},{8,39},{9,40},{10... | collective-permute-start | bytes 12296 | tf_op jit(solution)/shard_map/ppermute | solution.py:592
  11.3 11.1 %copy-start = (f32[8,32,4096]{2,1,0:T(8,128)}, f32[8,32,4096]{2,1,0:T(8,128)S(1)}, u32[]{:S(2)}) copy-start(f32[8,32,4096]{2,1,0:T(8,128)S(1)} %get-tuple-element.13.forcing_ref) | copy-start | bytes 12582916
  22.4 17.1 %all-to-all-start = ((f32[8,144,128]{2,1,0:T(8,128)}), f32[8,144,128]{2,1,0:T(8,128)S(1)}, u32[]{:S(2)}, u32[]{:S(2)}) async-start(f32[8,144,128]{2,1,0:T(8,128)} %get-tuple-element.20), calls=%async_computation | async-start | bytes 1179648 | tf_op jit(solution)/shard_map/all_to_all | solution.py:609
  25.9 25.1 %collective-permute-start.5 = (f32[32,4224]{1,0:T(8,128)S(1)}, f32[32,4224]{1,0:T(8,128)S(1)}, u32[]{:S(2)}, u32[]{:S(2)}) collective-permute-start(f32[32,4224]{1,0:T(8,128)S(1)} %get-tuple-element.19.value_ref), channel_id=1, source_target_pairs={{0,32},{32,64},{64,96},{96,128},{128,160},{160,192},{192,224},{224... | collective-permute-start | bytes 1622024 | tf_op jit(solution)/shard_map/ppermute | solution.py:610
  43.6 15.8 %all-to-all-start.1 = ((f32[8,128,128]{2,1,0:T(8,128)}), f32[8,128,128]{2,1,0:T(8,128)S(1)}, u32[]{:S(2)}, u32[]{:S(2)}) async-start(f32[8,128,128]{2,1,0:T(8,128)} %coarse_solve.1), calls=%async_computation.1 | async-start | bytes 1048576 | tf_op jit(solution)/shard_map/all_to_all | solution.py:612
  51.1 2.2 %copy-start.1 = (f32[8,32,4096]{2,1,0:T(8,128)S(1)}, f32[8,32,4096]{2,1,0:T(8,128)}, u32[]{:S(2)}) copy-start(f32[8,32,4096]{2,1,0:T(8,128)} %copy-done) | copy-start | bytes 12582916

commit v3 on v2

--- a/solution.py
+++ b/solution.py
@@ -7,11 +7,13 @@
 
 LANES = 128
 REACH = 32
+RIM = 8
 COND = 16
 ROWS = 2 * COND
 ONCE = 5 * COND
 TWICE = 9 * COND
 FINE, COARSE, COARSE_TWICE, OPERATORS = 0, ONCE, 2 * ONCE, 2 * ONCE + TWICE
+AHEAD = 3
 VMEM_LIMIT = 20 * 1024 * 1024
 
 
@@ -38,16 +40,6 @@
     lane = iota((ROWS, LANES), 1)
     right = jnp.where(lane < REACH, unpack_edge(from_right, 0), 0.0)
     return jnp.where(lane >= LANES - REACH, unpack_edge(from_left, LANES - REACH), right)
-
-
-def pack_halo(halo):
-    lane = iota((COND, LANES), 1)
-    outer = (lane < REACH) | (lane >= LANES - REACH)
-    return jnp.where(outer, halo[:COND], pltpu.roll(halo[COND:], LANES // 2, 1))
-
-
-def unpack_halo(packed):
-    return jnp.concatenate([packed, pltpu.roll(packed, LANES // 2, 1)], axis=0)
 
 
 def join_halo(right, left):
@@ -265,7 +257,7 @@
         for i in range(tiles):
             out_ref[j, at + ROWS * i : at + ROWS * (i + 1), :] = tile(j * tiles + i)
         rim = join_halo(tile((j + 1) * tiles), tile(j * tiles - 1))
-        out_ref[j, at + ROWS * tiles : at + ROWS * tiles + COND, :] = pack_halo(rim)
+        out_ref[j, at + ROWS * tiles : at + ROWS * tiles + RIM, :] = pack_edge(rim, LANES - REACH // 2)
 
 
 def source_halo_kernel(forcing_ref, left_ref, right_ref, halo_ref):
@@ -286,25 +278,6 @@
         compiler_params=pltpu.CompilerParams(vmem_limit_bytes=VMEM_LIMIT),
         name="source_halos",
     )(forcing, left, right)
-
-
-def start_chain(main_ref, begin_ref, initial_ref, sem):
-    is_first = lax.axis_index("tm") == 0
-
-    @pl.when(is_first)
-    def _():
-        pltpu.make_async_copy(initial_ref, main_ref, sem).start()
-
-    @pl.when(jnp.logical_not(is_first))
-    def _():
-        pltpu.make_async_copy(begin_ref, main_ref, sem).start()
-
-    return pltpu.make_async_copy(begin_ref, main_ref, sem)
-
-
-def halo_of(main_ref, from_left, from_right):
-    length = main_ref.shape[1]
-    return make_halo(from_left, from_right, main_ref[:, :LANES], main_ref[:, length - LANES :])
 
 
 def first_kernel(
@@ -383,7 +356,7 @@
     groups,
 ):
     steps, _, length = forcing.shape
-    rows = length // groups // LANES * ROWS + COND
+    rows = length // groups // LANES * ROWS + RIM
     anywhere = pl.BlockSpec(memory_space=pl.ANY)
     vmem = pl.BlockSpec(memory_space=pltpu.VMEM)
     return pl.pallas_call(
@@ -425,7 +398,7 @@
 
 def coarse_kernel(parts_ref, weights_ref, out_ref, even_ref, odd_ref):
     groups = parts_ref.shape[0]
-    tiles = (parts_ref.shape[1] - COND) // ROWS
+    tiles = (parts_ref.shape[1] - RIM) // ROWS
     width = (tiles + 1) * LANES
 
     states = (even_ref, odd_ref)
@@ -437,7 +410,7 @@
                     return tile_of(states[n % 2], t * (tiles + 1) + k)
                 if k < tiles:
                     return parts_ref[t, ROWS * k : ROWS * (k + 1), :]
-                return unpack_halo(parts_ref[t, ROWS * tiles : ROWS * tiles + COND, :])
+                return unpack_edge(parts_ref[t, ROWS * tiles : ROWS * tiles + RIM, :], LANES - REACH // 2)
 
             def store(k, tile, n=n, t=t):
                 at = t * width + k * LANES
@@ -469,7 +442,7 @@
 
 def coarse_solve(parts, weights):
     groups, rows, _ = parts.shape
-    tiles = (rows - COND) // ROWS
+    tiles = (rows - RIM) // ROWS
     return pl.pallas_call(
         coarse_kernel,
         out_shape=pltpu.VMEM((groups, ROWS * tiles, LANES), jnp.float32),
@@ -490,59 +463,91 @@
     weights_ref,
     out_ref,
     states_ref,
-    halo_ref,
-    sems,
+    source_ref,
+    low_ref,
+    high_ref,
+    source_sems,
     out_sems,
 ):
-    steps = out_sems.shape[0]
+    steps = states_ref.shape[0]
     length = forcing_ref.shape[2]
+    tiles = length // LANES
     initial_at = left_ref.shape[0] - 1
-    halo = pltpu.make_async_copy(begin_ref.at[:, length:], halo_ref, sems.at[1])
-    halo.start()
-    begun = start_chain(states_ref.at[0], begin_ref.at[:, :length], initial_ref, sems.at[0])
-    halo.wait()
-    begun.wait()
-
-    @pl.when(lax.axis_index("tm") == 0)
-    def _():
-        halo_ref[...] = halo_of(states_ref.at[0], left_ref[initial_at], right_ref[initial_at])
+    is_first = lax.axis_index("tm") == 0
+
+    def source(n):
+        return pltpu.make_async_copy(forcing_ref.at[n], source_ref.at[n], source_sems.at[n])
 
     def result(n):
-        return pltpu.make_async_copy(states_ref.at[n + 1], out_ref.at[n], out_sems.at[n])
-
-    def one(n, carry):
-        state = jnp.concatenate([states_ref[n], halo_ref[...]], axis=1)
-        state = step(state, weights_ref[FINE:COARSE], length + LANES)
-        states_ref[n + 1] = state[:, :length] + forcing_ref[n]
-        halo_ref[...] = state[:, length:] + source_halo_ref[n]
+        return pltpu.make_async_copy(states_ref.at[n], out_ref.at[n], out_sems.at[n])
+
+    for n in range(AHEAD):
+        source(n).start()
+
+    def begin(k):
+        return jnp.where(is_first, tile_of(initial_ref, k), tile_of(begin_ref, k))
+
+    begin_halo = jnp.where(
+        is_first,
+        make_halo(left_ref[initial_at], right_ref[initial_at], begin(0), begin(tiles - 1)),
+        tile_of(begin_ref, tiles),
+    )
+    for n in range(steps):
+        source(n).wait()
+        if n + AHEAD < steps:
+            source(n + AHEAD).start()
+
+        def load(k, n=n):
+            if 0 < k <= tiles:
+                return tile_of(states_ref.at[n - 1], k - 1) if n > 0 else begin(k - 1)
+            if n == 0:
+                return begin_halo
+            return low_ref[n - 1] if k == 0 else high_ref[n - 1]
+
+        def store(k, tile, n=n):
+            if 0 < k <= tiles:
+                states_ref[n, :, (k - 1) * LANES : k * LANES] = tile + tile_of(source_ref.at[n], k - 1)
+            elif k == 0:
+                low_ref[n] = tile + source_halo_ref[n]
+            else:
+                high_ref[n] = tile + source_halo_ref[n]
+
+        step_tiles(load, store, tiles + 2, weights_ref[FINE:COARSE], False, 2)
         result(n).start()
-        return carry
-
-    lax.fori_loop(0, steps, one, 0)
     for n in range(steps):
         result(n).wait()
 
 
 def second_chain(forcing, source_halo, begin, initial, left, right, weights):
     count, _, length = forcing.shape
+    steps = count - 1
     hbm = pl.BlockSpec(memory_space=pltpu.HBM)
-    anywhere = pl.BlockSpec(memory_space=pl.ANY)
     vmem = pl.BlockSpec(memory_space=pltpu.VMEM)
     return pl.pallas_call(
         second_kernel,
         out_shape=jax.ShapeDtypeStruct(forcing.shape, jnp.float32),
-        in_specs=[vmem, vmem, anywhere, anywhere, vmem, vmem, vmem],
+        in_specs=[hbm, vmem, vmem, vmem, vmem, vmem, vmem],
         out_specs=hbm,
         scratch_shapes=[
-            pltpu.VMEM(forcing.shape, jnp.float32),
-            pltpu.VMEM((ROWS, LANES), jnp.float32),
-            pltpu.SemaphoreType.DMA((2,)),
-            pltpu.SemaphoreType.DMA((count - 1,)),
+            pltpu.VMEM((steps, ROWS, length), jnp.float32),
+            pltpu.VMEM((steps, ROWS, length), jnp.float32),
+            pltpu.VMEM((steps, ROWS, LANES), jnp.float32),
+            pltpu.VMEM((steps, ROWS, LANES), jnp.float32),
+            pltpu.SemaphoreType.DMA((steps,)),
+            pltpu.SemaphoreType.DMA((steps,)),
         ],
         compiler_params=pltpu.CompilerParams(vmem_limit_bytes=VMEM_LIMIT),
         cost_estimate=cost(count, length, 2 * forcing.size),
         name="second_chain",
-    )(forcing, source_halo, begin, initial, left, right, weights)
+    )(
+        pltpu.with_memory_space_constraint(forcing, pltpu.HBM),
+        source_halo,
+        begin,
+        initial,
+        left,
+        right,
+        weights,
+    )
 
 
 def correct_kernel(value_ref, parts_ref, states_ref, out_ref):
@@ -610,7 +615,7 @@
     begin = lax.ppermute(value, "tm", to_next)
     parts = coarse_solve(parts, weights)
     parts = lax.all_to_all(parts, "tm", 0, 0, tiled=True)
-    states = second_chain(staged, source_halo, begin, initial, left, right, weights)
+    states = second_chain(forcing, source_halo, begin, initial, left, right, weights)
     return correct_last(value, parts, states)
 
 

time: 60.5 us -> 60.1 us (level)
  local copies, waits for them, and re-layouts: 2.21 us -> 0.01 us
  Pallas kernels: 17.5 us -> 18.4 us
  waiting for transfers between devices: 24.8 us -> 25.6 us
    unnamed x12 -> x8, local copies, waits for them, and re-layouts: 2.21 us -> 0.01 us
    pallas_call x1, Pallas kernels: 4.18 us -> 5.14 us  [second_chain(): pl.pallas_call(second_kernel, out_shape=jax.ShapeDtypeStruct(forcing.shap...]
    all_to_all x2, waiting for transfers between devices: 13.5 us -> 14.4 us  [body(): parts = lax.all_to_all(parts, 'tm', 0, 0, tiled=True)]
  transfers between devices with their start and end apart: 8 -> 8, of which waited for: 4 -> 4; matrix products, arithmetic and copies ran while one was open for 0% -> 0% of each run, Pallas kernels for 22% -> 24%
where the time goes in v3:
time: 60.1 us; the launch traced here: 59.8 us
  waiting for transfers between devices  25.6 us (43%)
  Pallas kernels  18.4 us (31%)
  starting transfers between devices  15.7 us (26%)
    all_to_all x2, waiting for transfers between devices, body(): parts = lax.all_to_all(parts, 'tm', 0, 0, tiled=True)  14.4 us
    ppermute x1, waiting for transfers between devices, body(): left = lax.ppermute(high, 'space', up)  7.31 us
    all_to_all x2, starting transfers between devices, body(): parts = lax.all_to_all(parts, 'tm', 0, 0, tiled=True)  7.22 us
    pallas_call x1, Pallas kernels, second_chain(): pl.pallas_call(second_kernel, out_shape=jax.ShapeDtypeStruct(forcing.shap...  5.14 us
    pallas_call x1, Pallas kernels, coarse_solve(): pl.pallas_call(coarse_kernel, out_shape=pltpu.VMEM((groups, ROWS * tiles,...  4.04 us
    ppermute x1, waiting for transfers between devices, body(): begin = lax.ppermute(value, 'tm', to_next)  3.86 us
    pallas_call x1, Pallas kernels, first_chain(): pl.pallas_call(first_kernel, out_shape=(pltpu.VMEM((groups, rows, LANES),...  3.47 us
    pallas_call x1, Pallas kernels, prepare(): pl.pallas_call(prepare_kernel, out_shape=(pltpu.VMEM((OPERATORS, 4 * ROWS...  2.94 us
  transfers between devices with their start and end apart: 8, of which 4 were waited for; matrix products, arithmetic and copies ran while one was open for 0% of the time, Pallas kernels for 24%

profile of v3, /device:TPU:104, one launch (start us, length us, event | category | flops | bytes accessed | tf_op | source)
XLA Modules:
  0.0 59.8 jit_solution(4254506107431953747)
XLA Ops:
  0.0 0.0 copy-start.2
  0.0 0.0 copy-start.3
  0.0 1.5 %collective-permute-start.2 = (f32[32,4096]{1,0:T(8,128)}, f32[32,4096]{1,0:T(8,128)S(1)}, u32[]{:S(2)}, u32[]{:S(2)}) collective-permute-start(f32[32,4096]{1,0:T(8,128)} %bitcast.1), channel_id=1, source_target_pairs={{0,32},{32,64},{64,96},{96,128},{128,160},{160,192},{192,224},{224... | collective-permute-start | bytes 1572872 | tf_op jit(solution)/shard_map/ppermute | solution.py:593
  1.5 1.8 %edges.1 = (f32[10,8,128]{2,1,0:T(8,128)}, f32[10,8,128]{2,1,0:T(8,128)}, f32[8,128]{1,0:T(8,128)}, f32[8,128]{1,0:T(8,128)}) custom-call(f32[8,32,4096]{2,1,0:T(8,128)} %forcing_ref.3, f32[8,32,4096]{2,1,0:T(8,128)} %forcing_ref.3, f32[1,32,4096]{2,1,0:T(8,128)} %guess_ref.1, f32[1,32,4096]{2,1,0:T(8,128)} %guess_ref.1, f32[32,4096]{1,0:T(8,128)} %initial_ref.3, ...), custom_call_target="tpu_custom_call" | custom-call | tf_op jit(solution)/shard_map/edges/pallas_call | solution.py:233
  3.2 0.0 collective-permute-start
  3.3 1.7 %collective-permute-start.1 = (f32[10,8,128]{2,1,0:T(8,128)}, f32[10,8,128]{2,1,0:T(8,128)S(1)}, u32[]{:S(2)}, u32[]{:S(2)}) collective-permute-start(f32[10,8,128]{2,1,0:T(8,128)} %get-tuple-element.15), channel_id=1, source_target_pairs={{1,0},{2,1},{3,2},{4,3},{5,4},{6,5},{7,6},{8,7},{9,8},{10,9},{11,1... | collective-permute-start | bytes 122888 | tf_op jit(solution)/shard_map/ppermute | solution.py:595
  5.0 2.5 %collective-permute-start.3 = (f32[8,128]{1,0:T(8,128)}, f32[8,128]{1,0:T(8,128)S(1)}, u32[]{:S(2)}, u32[]{:S(2)}) collective-permute-start(f32[8,128]{1,0:T(8,128)} %get-tuple-element.16), channel_id=1, source_target_pairs={{0,33},{1,34},{2,35},{3,36},{4,37},{5,38},{6,39},{7,40},{8,41},{9,... | collective-permute-start | bytes 12296 | tf_op jit(solution)/shard_map/ppermute | solution.py:598
  7.5 0.0 copy-start
  7.5 0.0 copy-start.1
  7.5 0.8 %collective-permute-start.4 = (f32[8,128]{1,0:T(8,128)}, f32[8,128]{1,0:T(8,128)S(1)}, u32[]{:S(2)}, u32[]{:S(2)}) collective-permute-start(f32[8,128]{1,0:T(8,128)} %get-tuple-element.17), channel_id=1, source_target_pairs={{1,32},{2,33},{3,34},{4,35},{5,36},{6,37},{7,38},{8,39},{9,40},{10... | collective-permute-start | bytes 12296 | tf_op jit(solution)/shard_map/ppermute | solution.py:597
  8.3 0.0 copy-done.2
  8.3 0.0 copy-done.3
  8.3 2.9 %prepare.1 = (bf16[304,128]{1,0:T(8,128)(2,1)S(1)}, f32[8,32,4096]{2,1,0:T(8,128)S(1)}) custom-call(f32[4,16,16]{2,1,0:T(8,128)S(1)} %copy-done.2, f32[4,16,16]{2,1,0:T(8,128)S(1)} %copy-done.3, f32[8,32,4096]{2,1,0:T(8,128)} %forcing_ref.3), custom_call_target="tpu_custom_call" | custom-call | tf_op jit(solution)/shard_map/prepare/pallas_call | solution.py:193
  11.3 7.3 %collective-permute-done.left_ref = f32[10,8,128]{2,1,0:T(8,128)S(1)} collective-permute-done((f32[10,8,128]{2,1,0:T(8,128)}, f32[10,8,128]{2,1,0:T(8,128)S(1)}, u32[]{:S(2)}, u32[]{:S(2)}) %collective-permute-start) | collective-permute-done | bytes 40992 | tf_op jit(solution)/shard_map/ppermute | solution.py:596
  18.6 0.0 collective-permute-done.1.right_ref
  18.6 0.2 source_halos.1.source_halo_ref
  18.8 0.0 collective-permute-done.3.begin_left_ref
  18.8 0.0 collective-permute-done.4.begin_right_ref
  18.9 0.0 collective-permute-done.2.begin_ref
  18.9 0.0 copy-done
  18.9 0.0 copy-done.1
  18.9 3.5 %first_chain.1 = (f32[8,136,128]{2,1,0:T(8,128)}, f32[32,4224]{1,0:T(8,128)S(1)}) custom-call(f32[8,32,4096]{2,1,0:T(8,128)S(1)} %get-tuple-element.13.forcing_ref, f32[8,32,128]{2,1,0:T(8,128)S(1)} %source_halos.1.source_halo_ref, f32[32,4096]{1,0:T(8,128)S(1)} %collective-permute-done.2.begin_ref, f32[32,4096]{1,0:T(8,128)S(1)} %copy-done.1, ...), custom_call_target="tpu_custom_call" | custom-call | flops 5368709120 | bytes 8388608 | tf_op jit(solution)/shard_map/first_chain/pallas_call | solution.py:362
  22.4 3.5 %all-to-all-start = ((f32[8,136,128]{2,1,0:T(8,128)}), f32[8,136,128]{2,1,0:T(8,128)S(1)}, u32[]{:S(2)}, u32[]{:S(2)}) async-start(f32[8,136,128]{2,1,0:T(8,128)} %get-tuple-element.20), calls=%async_computation | async-start | bytes 1114112 | tf_op jit(solution)/shard_map/all_to_all | solution.py:614
  25.9 1.9 %collective-permute-start.5 = (f32[32,4224]{1,0:T(8,128)S(1)}, f32[32,4224]{1,0:T(8,128)S(1)}, u32[]{:S(2)}, u32[]{:S(2)}) collective-permute-start(f32[32,4224]{1,0:T(8,128)S(1)} %get-tuple-element.19.value_ref), channel_id=1, source_target_pairs={{0,32},{32,64},{64,96},{96,128},{128,160},{160,192},{192,224},{224... | collective-permute-start | bytes 1622024 | tf_op jit(solution)/shard_map/ppermute | solution.py:615
  27.8 11.3 %all-to-all-done.parts_ref = f32[8,136,128]{2,1,0:T(8,128)S(1)} async-done(((f32[8,136,128]{2,1,0:T(8,128)}), f32[8,136,128]{2,1,0:T(8,128)S(1)}, u32[]{:S(2)}, u32[]{:S(2)}) %all-to-all-start) | async-done | bytes 557088 | tf_op jit(solution)/shard_map/all_to_all | solution.py:614
  39.1 4.0 %coarse_solve.1 = f32[8,128,128]{2,1,0:T(8,128)} custom-call(f32[8,136,128]{2,1,0:T(8,128)S(1)} %all-to-all-done.parts_ref, bf16[304,128]{1,0:T(8,128)(2,1)S(1)} %get-tuple-element.18.weights_ref), custom_call_target="tpu_custom_call" | custom-call | flops 8053063680 | bytes 1114112 | tf_op jit(solution)/shard_map/coarse_solve/pallas_call | solution.py:446
  43.1 3.7 %all-to-all-start.1 = ((f32[8,128,128]{2,1,0:T(8,128)}), f32[8,128,128]{2,1,0:T(8,128)S(1)}, u32[]{:S(2)}, u32[]{:S(2)}) async-start(f32[8,128,128]{2,1,0:T(8,128)} %coarse_solve.1), calls=%async_computation.1 | async-start | bytes 1048576 | tf_op jit(solution)/shard_map/all_to_all | solution.py:617
  46.8 3.9 %collective-permute-done.5.begin_ref = f32[32,4224]{1,0:T(8,128)S(1)} collective-permute-done((f32[32,4224]{1,0:T(8,128)S(1)}, f32[32,4224]{1,0:T(8,128)S(1)}, u32[]{:S(2)}, u32[]{:S(2)}) %collective-permute-start.5) | collective-permute-done | bytes 540704 | tf_op jit(solution)/shard_map/ppermute | solution.py:615
  50.7 5.1 %second_chain.1.states_ref = f32[8,32,4096]{2,1,0:T(8,128)} custom-call(f32[8,32,4096]{2,1,0:T(8,128)} %forcing_ref.3, f32[8,32,128]{2,1,0:T(8,128)S(1)} %source_halos.1.source_halo_ref, f32[32,4224]{1,0:T(8,128)S(1)} %collective-permute-done.5.begin_ref, f32[32,4096]{1,0:T(8,128)S(1)} %copy-done.1, f32[10,8,128]{2,1,0:T(8,128)S(1)} %collective-permute-done.left_ref, ...), custom_call_target="tpu_custom_call" | custom-call | flops 5368709120 | bytes 16777216 | tf_op jit(solution)/shard_map/second_chain/pallas_call | solution.py:526
  55.8 3.1 %all-to-all-done.1.parts_ref = f32[8,128,128]{2,1,0:T(8,128)S(1)} async-done(((f32[8,128,128]{2,1,0:T(8,128)}), f32[8,128,128]{2,1,0:T(8,128)S(1)}, u32[]{:S(2)}, u32[]{:S(2)}) %all-to-all-start.1) | async-done | bytes 524320 | tf_op jit(solution)/shard_map/all_to_all | solution.py:617
  58.9 0.8 %correct_last.1 = f32[8,32,4096]{2,1,0:T(8,128)} custom-call(f32[32,4224]{1,0:T(8,128)S(1)} %get-tuple-element.19.value_ref, f32[8,128,128]{2,1,0:T(8,128)S(1)} %all-to-all-done.1.parts_ref, f32[8,32,4096]{2,1,0:T(8,128)} %second_chain.1.states_ref), custom_call_target="tpu_custom_call", output_to_operand_aliasing={{}: (2, {})} | custom-call | tf_op jit(solution)/shard_map/correct_last/pallas_call | solution.py:567
Async XLA Ops:
  0.0 8.3 %copy-start.2 = (f32[4,16,16]{2,1,0:T(8,128)S(1)}, f32[4,16,16]{2,1,0:T(8,128)}, u32[]{:S(2)}) copy-start(f32[4,16,16]{2,1,0:T(8,128)} %fine_ref.1) | copy-start | bytes 12292
  0.0 8.3 %copy-start.3 = (f32[4,16,16]{2,1,0:T(8,128)S(1)}, f32[4,16,16]{2,1,0:T(8,128)}, u32[]{:S(2)}) copy-start(f32[4,16,16]{2,1,0:T(8,128)} %coarse_ref.1) | copy-start | bytes 12292
  0.0 18.9 %collective-permute-start.2 = (f32[32,4096]{1,0:T(8,128)}, f32[32,4096]{1,0:T(8,128)S(1)}, u32[]{:S(2)}, u32[]{:S(2)}) collective-permute-start(f32[32,4096]{1,0:T(8,128)} %bitcast.1), channel_id=1, source_target_pairs={{0,32},{32,64},{64,96},{96,128},{128,160},{160,192},{192,224},{224... | collective-permute-start | bytes 1572872 | tf_op jit(solution)/shard_map/ppermute | solution.py:593
  3.2 15.3 %collective-permute-start = (f32[10,8,128]{2,1,0:T(8,128)}, f32[10,8,128]{2,1,0:T(8,128)S(1)}, u32[]{:S(2)}, u32[]{:S(2)}) collective-permute-start(f32[10,8,128]{2,1,0:T(8,128)} %get-tuple-element.14), channel_id=1, source_target_pairs={{0,1},{1,2},{2,3},{3,4},{4,5},{5,6},{6,7},{7,8},{8,9},{9,10},{10,1... | collective-permute-start | bytes 122888 | tf_op jit(solution)/shard_map/ppermute | solution.py:596
  3.3 15.3 %collective-permute-start.1 = (f32[10,8,128]{2,1,0:T(8,128)}, f32[10,8,128]{2,1,0:T(8,128)S(1)}, u32[]{:S(2)}, u32[]{:S(2)}) collective-permute-start(f32[10,8,128]{2,1,0:T(8,128)} %get-tuple-element.15), channel_id=1, source_target_pairs={{1,0},{2,1},{3,2},{4,3},{5,4},{6,5},{7,6},{8,7},{9,8},{10,9},{11,1... | collective-permute-start | bytes 122888 | tf_op jit(solution)/shard_map/ppermute | solution.py:595
  5.0 13.8 %collective-permute-start.3 = (f32[8,128]{1,0:T(8,128)}, f32[8,128]{1,0:T(8,128)S(1)}, u32[]{:S(2)}, u32[]{:S(2)}) collective-permute-start(f32[8,128]{1,0:T(8,128)} %get-tuple-element.16), channel_id=1, source_target_pairs={{0,33},{1,34},{2,35},{3,36},{4,37},{5,38},{6,39},{7,40},{8,41},{9,... | collective-permute-start | bytes 12296 | tf_op jit(solution)/shard_map/ppermute | solution.py:598
  7.5 11.4 %copy-start = (f32[1,32,4096]{2,1,0:T(8,128)S(1)}, f32[1,32,4096]{2,1,0:T(8,128)}, u32[]{:S(2)}) copy-start(f32[1,32,4096]{2,1,0:T(8,128)} %guess_ref.1) | copy-start | bytes 1572868
  7.5 11.4 %copy-start.1 = (f32[32,4096]{1,0:T(8,128)S(1)}, f32[32,4096]{1,0:T(8,128)}, u32[]{:S(2)}) copy-start(f32[32,4096]{1,0:T(8,128)} %initial_ref.3) | copy-start | bytes 1572868
  7.5 11.4 %collective-permute-start.4 = (f32[8,128]{1,0:T(8,128)}, f32[8,128]{1,0:T(8,128)S(1)}, u32[]{:S(2)}, u32[]{:S(2)}) collective-permute-start(f32[8,128]{1,0:T(8,128)} %get-tuple-element.17), channel_id=1, source_target_pairs={{1,32},{2,33},{3,34},{4,35},{5,36},{6,37},{7,38},{8,39},{9,40},{10... | collective-permute-start | bytes 12296 | tf_op jit(solution)/shard_map/ppermute | solution.py:597
  22.4 16.7 %all-to-all-start = ((f32[8,136,128]{2,1,0:T(8,128)}), f32[8,136,128]{2,1,0:T(8,128)S(1)}, u32[]{:S(2)}, u32[]{:S(2)}) async-start(f32[8,136,128]{2,1,0:T(8,128)} %get-tuple-element.20), calls=%async_computation | async-start | bytes 1114112 | tf_op jit(solution)/shard_map/all_to_all | solution.py:614
  25.9 24.8 %collective-permute-start.5 = (f32[32,4224]{1,0:T(8,128)S(1)}, f32[32,4224]{1,0:T(8,128)S(1)}, u32[]{:S(2)}, u32[]{:S(2)}) collective-permute-start(f32[32,4224]{1,0:T(8,128)S(1)} %get-tuple-element.19.value_ref), channel_id=1, source_target_pairs={{0,32},{32,64},{64,96},{96,128},{128,160},{160,192},{192,224},{224... | collective-permute-start | bytes 1622024 | tf_op jit(solution)/shard_map/ppermute | solution.py:615
  43.1 15.8 %all-to-all-start.1 = ((f32[8,128,128]{2,1,0:T(8,128)}), f32[8,128,128]{2,1,0:T(8,128)S(1)}, u32[]{:S(2)}, u32[]{:S(2)}) async-start(f32[8,128,128]{2,1,0:T(8,128)} %coarse_solve.1), calls=%async_computation.1 | async-start | bytes 1048576 | tf_op jit(solution)/shard_map/all_to_all | solution.py:617

commit v4 on v3

--- a/solution.py
+++ b/solution.py
@@ -330,7 +330,7 @@
             else:
                 states[(n + 1) % 2][:, k * LANES : (k + 1) * LANES] = tile
 
-        step_tiles(load, store, tiles + 2, weights_ref[FINE:COARSE], False, 2)
+        step_tiles(load, store, tiles + 2, weights_ref[FINE:COARSE], False, 3)
 
     end = states[steps % 2]
     halo = join_halo(tile_of(end, tiles + 1), tile_of(end, 0))
@@ -512,7 +512,7 @@
             else:
                 high_ref[n] = tile + source_halo_ref[n]
 
-        step_tiles(load, store, tiles + 2, weights_ref[FINE:COARSE], False, 2)
+        step_tiles(load, store, tiles + 2, weights_ref[FINE:COARSE], False, 3)
         result(n).start()
     for n in range(steps):
         result(n).wait()
@@ -612,7 +612,7 @@
         groups,
     )
     parts = lax.all_to_all(parts, "tm", 0, 0, tiled=True)
-    begin = lax.ppermute(value, "tm", to_next)
+    begin = lax.ppermute(value, "tm", to_next[:-1])
     parts = coarse_solve(parts, weights)
     parts = lax.all_to_all(parts, "tm", 0, 0, tiled=True)
     states = second_chain(forcing, source_halo, begin, initial, left, right, weights)

time: 60.1 us -> 59.8 us (level)
  waiting for transfers between devices: 25.6 us -> 23.2 us
  starting transfers between devices: 15.7 us -> 17.6 us
    ppermute x1, waiting for transfers between devices: 3.86 us -> 0.01 us  [body(): begin = lax.ppermute(value, 'tm', to_next[:-1])]
    ppermute x1, starting transfers between devices: 1.92 us -> 3.85 us  [body(): begin = lax.ppermute(value, 'tm', to_next[:-1])]
    all_to_all x2, waiting for transfers between devices: 14.4 us -> 15.8 us  [body(): parts = lax.all_to_all(parts, 'tm', 0, 0, tiled=True)]
  transfers between devices with their start and end apart: 8 -> 8, of which waited for: 4 -> 3; matrix products, arithmetic and copies ran while one was open for 0% -> 0% of each run, Pallas kernels for 24% -> 24%
where the time goes in v4:
time: 59.8 us; the launch traced here: 59.5 us
  waiting for transfers between devices  23.2 us (39%)
  Pallas kernels  18.5 us (31%)
  starting transfers between devices  17.6 us (29%)
    all_to_all x2, waiting for transfers between devices, body(): parts = lax.all_to_all(parts, 'tm', 0, 0, tiled=True)  15.8 us
    ppermute x1, waiting for transfers between devices, body(): left = lax.ppermute(high, 'space', up)  7.31 us
    all_to_all x2, starting transfers between devices, body(): parts = lax.all_to_all(parts, 'tm', 0, 0, tiled=True)  7.22 us
    pallas_call x1, Pallas kernels, second_chain(): pl.pallas_call(second_kernel, out_shape=jax.ShapeDtypeStruct(forcing.shap...  5.37 us
    pallas_call x1, Pallas kernels, coarse_solve(): pl.pallas_call(coarse_kernel, out_shape=pltpu.VMEM((groups, ROWS * tiles,...  4.05 us
    ppermute x1, starting transfers between devices, body(): begin = lax.ppermute(value, 'tm', to_next[:-1])  3.85 us
    pallas_call x1, Pallas kernels, first_chain(): pl.pallas_call(first_kernel, out_shape=(pltpu.VMEM((groups, rows, LANES),...  3.34 us
    pallas_call x1, Pallas kernels, prepare(): pl.pallas_call(prepare_kernel, out_shape=(pltpu.VMEM((OPERATORS, 4 * ROWS...  2.94 us
  transfers between devices with their start and end apart: 8, of which 3 were waited for; matrix products, arithmetic and copies ran while one was open for 0% of the time, Pallas kernels for 24%

profile of v4, /device:TPU:104, one launch (start us, length us, event | category | flops | bytes accessed | tf_op | source)
XLA Modules:
  0.0 59.5 jit_solution(13555814645735098070)
XLA Ops:
  0.0 0.0 copy-start.2
  0.0 0.0 copy-start.3
  0.0 1.5 %collective-permute-start.2 = (f32[32,4096]{1,0:T(8,128)}, f32[32,4096]{1,0:T(8,128)S(1)}, u32[]{:S(2)}, u32[]{:S(2)}) collective-permute-start(f32[32,4096]{1,0:T(8,128)} %bitcast.1), channel_id=1, source_target_pairs={{0,32},{32,64},{64,96},{96,128},{128,160},{160,192},{192,224},{224... | collective-permute-start | bytes 1572872 | tf_op jit(solution)/shard_map/ppermute | solution.py:593
  1.5 1.8 %edges.1 = (f32[10,8,128]{2,1,0:T(8,128)}, f32[10,8,128]{2,1,0:T(8,128)}, f32[8,128]{1,0:T(8,128)}, f32[8,128]{1,0:T(8,128)}) custom-call(f32[8,32,4096]{2,1,0:T(8,128)} %forcing_ref.3, f32[8,32,4096]{2,1,0:T(8,128)} %forcing_ref.3, f32[1,32,4096]{2,1,0:T(8,128)} %guess_ref.1, f32[1,32,4096]{2,1,0:T(8,128)} %guess_ref.1, f32[32,4096]{1,0:T(8,128)} %initial_ref.3, ...), custom_call_target="tpu_custom_call" | custom-call | tf_op jit(solution)/shard_map/edges/pallas_call | solution.py:233
  3.2 0.0 collective-permute-start
  3.3 1.7 %collective-permute-start.1 = (f32[10,8,128]{2,1,0:T(8,128)}, f32[10,8,128]{2,1,0:T(8,128)S(1)}, u32[]{:S(2)}, u32[]{:S(2)}) collective-permute-start(f32[10,8,128]{2,1,0:T(8,128)} %get-tuple-element.15), channel_id=1, source_target_pairs={{1,0},{2,1},{3,2},{4,3},{5,4},{6,5},{7,6},{8,7},{9,8},{10,9},{11,1... | collective-permute-start | bytes 122888 | tf_op jit(solution)/shard_map/ppermute | solution.py:595
  5.0 2.5 %collective-permute-start.3 = (f32[8,128]{1,0:T(8,128)}, f32[8,128]{1,0:T(8,128)S(1)}, u32[]{:S(2)}, u32[]{:S(2)}) collective-permute-start(f32[8,128]{1,0:T(8,128)} %get-tuple-element.16), channel_id=1, source_target_pairs={{0,33},{1,34},{2,35},{3,36},{4,37},{5,38},{6,39},{7,40},{8,41},{9,... | collective-permute-start | bytes 12296 | tf_op jit(solution)/shard_map/ppermute | solution.py:598
  7.5 0.0 copy-start
  7.5 0.0 copy-start.1
  7.5 0.8 %collective-permute-start.4 = (f32[8,128]{1,0:T(8,128)}, f32[8,128]{1,0:T(8,128)S(1)}, u32[]{:S(2)}, u32[]{:S(2)}) collective-permute-start(f32[8,128]{1,0:T(8,128)} %get-tuple-element.17), channel_id=1, source_target_pairs={{1,32},{2,33},{3,34},{4,35},{5,36},{6,37},{7,38},{8,39},{9,40},{10... | collective-permute-start | bytes 12296 | tf_op jit(solution)/shard_map/ppermute | solution.py:597
  8.3 0.0 copy-done.2
  8.3 0.0 copy-done.3
  8.3 2.9 %prepare.1 = (bf16[304,128]{1,0:T(8,128)(2,1)S(1)}, f32[8,32,4096]{2,1,0:T(8,128)S(1)}) custom-call(f32[4,16,16]{2,1,0:T(8,128)S(1)} %copy-done.2, f32[4,16,16]{2,1,0:T(8,128)S(1)} %copy-done.3, f32[8,32,4096]{2,1,0:T(8,128)} %forcing_ref.3), custom_call_target="tpu_custom_call" | custom-call | tf_op jit(solution)/shard_map/prepare/pallas_call | solution.py:193
  11.3 7.3 %collective-permute-done.left_ref = f32[10,8,128]{2,1,0:T(8,128)S(1)} collective-permute-done((f32[10,8,128]{2,1,0:T(8,128)}, f32[10,8,128]{2,1,0:T(8,128)S(1)}, u32[]{:S(2)}, u32[]{:S(2)}) %collective-permute-start) | collective-permute-done | bytes 40992 | tf_op jit(solution)/shard_map/ppermute | solution.py:596
  18.6 0.0 collective-permute-done.1.right_ref
  18.6 0.2 source_halos.1.source_halo_ref
  18.8 0.0 collective-permute-done.3.begin_left_ref
  18.8 0.0 collective-permute-done.4.begin_right_ref
  18.9 0.0 collective-permute-done.2.begin_ref
  18.9 0.0 copy-done
  18.9 0.0 copy-done.1
  18.9 3.3 %first_chain.1 = (f32[8,136,128]{2,1,0:T(8,128)}, f32[32,4224]{1,0:T(8,128)S(1)}) custom-call(f32[8,32,4096]{2,1,0:T(8,128)S(1)} %get-tuple-element.13.forcing_ref, f32[8,32,128]{2,1,0:T(8,128)S(1)} %source_halos.1.source_halo_ref, f32[32,4096]{1,0:T(8,128)S(1)} %collective-permute-done.2.begin_ref, f32[32,4096]{1,0:T(8,128)S(1)} %copy-done.1, ...), custom_call_target="tpu_custom_call" | custom-call | flops 5368709120 | bytes 8388608 | tf_op jit(solution)/shard_map/first_chain/pallas_call | solution.py:362
  22.2 3.5 %all-to-all-start = ((f32[8,136,128]{2,1,0:T(8,128)}), f32[8,136,128]{2,1,0:T(8,128)S(1)}, u32[]{:S(2)}, u32[]{:S(2)}) async-start(f32[8,136,128]{2,1,0:T(8,128)} %get-tuple-element.20), calls=%async_computation | async-start | bytes 1114112 | tf_op jit(solution)/shard_map/all_to_all | solution.py:614
  25.8 3.8 %collective-permute-start.5 = (f32[32,4224]{1,0:T(8,128)S(1)}, f32[32,4224]{1,0:T(8,128)S(1)}, u32[]{:S(2)}, u32[]{:S(2)}) collective-permute-start(f32[32,4224]{1,0:T(8,128)S(1)} %get-tuple-element.19.value_ref), channel_id=1, source_target_pairs={{0,32},{32,64},{64,96},{96,128},{128,160},{160,192},{192,224},{1,3... | collective-permute-start | bytes 1622024 | tf_op jit(solution)/shard_map/ppermute | solution.py:615
  29.6 9.3 %all-to-all-done.parts_ref = f32[8,136,128]{2,1,0:T(8,128)S(1)} async-done(((f32[8,136,128]{2,1,0:T(8,128)}), f32[8,136,128]{2,1,0:T(8,128)S(1)}, u32[]{:S(2)}, u32[]{:S(2)}) %all-to-all-start) | async-done | bytes 557088 | tf_op jit(solution)/shard_map/all_to_all | solution.py:614
  39.0 4.0 %coarse_solve.1 = f32[8,128,128]{2,1,0:T(8,128)} custom-call(f32[8,136,128]{2,1,0:T(8,128)S(1)} %all-to-all-done.parts_ref, bf16[304,128]{1,0:T(8,128)(2,1)S(1)} %get-tuple-element.18.weights_ref), custom_call_target="tpu_custom_call" | custom-call | flops 8053063680 | bytes 1114112 | tf_op jit(solution)/shard_map/coarse_solve/pallas_call | solution.py:446
  43.0 3.7 %all-to-all-start.1 = ((f32[8,128,128]{2,1,0:T(8,128)}), f32[8,128,128]{2,1,0:T(8,128)S(1)}, u32[]{:S(2)}, u32[]{:S(2)}) async-start(f32[8,128,128]{2,1,0:T(8,128)} %coarse_solve.1), calls=%async_computation.1 | async-start | bytes 1048576 | tf_op jit(solution)/shard_map/all_to_all | solution.py:617
  46.7 0.0 collective-permute-done.5.begin_ref
  46.7 5.4 %second_chain.1.states_ref = f32[8,32,4096]{2,1,0:T(8,128)} custom-call(f32[8,32,4096]{2,1,0:T(8,128)} %forcing_ref.3, f32[8,32,128]{2,1,0:T(8,128)S(1)} %source_halos.1.source_halo_ref, f32[32,4224]{1,0:T(8,128)S(1)} %collective-permute-done.5.begin_ref, f32[32,4096]{1,0:T(8,128)S(1)} %copy-done.1, f32[10,8,128]{2,1,0:T(8,128)S(1)} %collective-permute-done.left_ref, ...), custom_call_target="tpu_custom_call" | custom-call | flops 5368709120 | bytes 16777216 | tf_op jit(solution)/shard_map/second_chain/pallas_call | solution.py:526
  52.1 6.5 %all-to-all-done.1.parts_ref = f32[8,128,128]{2,1,0:T(8,128)S(1)} async-done(((f32[8,128,128]{2,1,0:T(8,128)}), f32[8,128,128]{2,1,0:T(8,128)S(1)}, u32[]{:S(2)}, u32[]{:S(2)}) %all-to-all-start.1) | async-done | bytes 524320 | tf_op jit(solution)/shard_map/all_to_all | solution.py:617
  58.6 0.8 %correct_last.1 = f32[8,32,4096]{2,1,0:T(8,128)} custom-call(f32[32,4224]{1,0:T(8,128)S(1)} %get-tuple-element.19.value_ref, f32[8,128,128]{2,1,0:T(8,128)S(1)} %all-to-all-done.1.parts_ref, f32[8,32,4096]{2,1,0:T(8,128)} %second_chain.1.states_ref), custom_call_target="tpu_custom_call", output_to_operand_aliasing={{}: (2, {})} | custom-call | tf_op jit(solution)/shard_map/correct_last/pallas_call | solution.py:567
Async XLA Ops:
  0.0 8.3 %copy-start.2 = (f32[4,16,16]{2,1,0:T(8,128)S(1)}, f32[4,16,16]{2,1,0:T(8,128)}, u32[]{:S(2)}) copy-start(f32[4,16,16]{2,1,0:T(8,128)} %fine_ref.1) | copy-start | bytes 12292
  0.0 8.3 %copy-start.3 = (f32[4,16,16]{2,1,0:T(8,128)S(1)}, f32[4,16,16]{2,1,0:T(8,128)}, u32[]{:S(2)}) copy-start(f32[4,16,16]{2,1,0:T(8,128)} %coarse_ref.1) | copy-start | bytes 12292
  0.0 18.9 %collective-permute-start.2 = (f32[32,4096]{1,0:T(8,128)}, f32[32,4096]{1,0:T(8,128)S(1)}, u32[]{:S(2)}, u32[]{:S(2)}) collective-permute-start(f32[32,4096]{1,0:T(8,128)} %bitcast.1), channel_id=1, source_target_pairs={{0,32},{32,64},{64,96},{96,128},{128,160},{160,192},{192,224},{224... | collective-permute-start | bytes 1572872 | tf_op jit(solution)/shard_map/ppermute | solution.py:593
  3.2 15.3 %collective-permute-start = (f32[10,8,128]{2,1,0:T(8,128)}, f32[10,8,128]{2,1,0:T(8,128)S(1)}, u32[]{:S(2)}, u32[]{:S(2)}) collective-permute-start(f32[10,8,128]{2,1,0:T(8,128)} %get-tuple-element.14), channel_id=1, source_target_pairs={{0,1},{1,2},{2,3},{3,4},{4,5},{5,6},{6,7},{7,8},{8,9},{9,10},{10,1... | collective-permute-start | bytes 122888 | tf_op jit(solution)/shard_map/ppermute | solution.py:596
  3.3 15.3 %collective-permute-start.1 = (f32[10,8,128]{2,1,0:T(8,128)}, f32[10,8,128]{2,1,0:T(8,128)S(1)}, u32[]{:S(2)}, u32[]{:S(2)}) collective-permute-start(f32[10,8,128]{2,1,0:T(8,128)} %get-tuple-element.15), channel_id=1, source_target_pairs={{1,0},{2,1},{3,2},{4,3},{5,4},{6,5},{7,6},{8,7},{9,8},{10,9},{11,1... | collective-permute-start | bytes 122888 | tf_op jit(solution)/shard_map/ppermute | solution.py:595
  5.0 13.8 %collective-permute-start.3 = (f32[8,128]{1,0:T(8,128)}, f32[8,128]{1,0:T(8,128)S(1)}, u32[]{:S(2)}, u32[]{:S(2)}) collective-permute-start(f32[8,128]{1,0:T(8,128)} %get-tuple-element.16), channel_id=1, source_target_pairs={{0,33},{1,34},{2,35},{3,36},{4,37},{5,38},{6,39},{7,40},{8,41},{9,... | collective-permute-start | bytes 12296 | tf_op jit(solution)/shard_map/ppermute | solution.py:598
  7.5 11.4 %copy-start = (f32[1,32,4096]{2,1,0:T(8,128)S(1)}, f32[1,32,4096]{2,1,0:T(8,128)}, u32[]{:S(2)}) copy-start(f32[1,32,4096]{2,1,0:T(8,128)} %guess_ref.1) | copy-start | bytes 1572868
  7.5 11.4 %copy-start.1 = (f32[32,4096]{1,0:T(8,128)S(1)}, f32[32,4096]{1,0:T(8,128)}, u32[]{:S(2)}) copy-start(f32[32,4096]{1,0:T(8,128)} %initial_ref.3) | copy-start | bytes 1572868
  7.5 11.4 %collective-permute-start.4 = (f32[8,128]{1,0:T(8,128)}, f32[8,128]{1,0:T(8,128)S(1)}, u32[]{:S(2)}, u32[]{:S(2)}) collective-permute-start(f32[8,128]{1,0:T(8,128)} %get-tuple-element.17), channel_id=1, source_target_pairs={{1,32},{2,33},{3,34},{4,35},{5,36},{6,37},{7,38},{8,39},{9,40},{10... | collective-permute-start | bytes 12296 | tf_op jit(solution)/shard_map/ppermute | solution.py:597
  22.2 16.7 %all-to-all-start = ((f32[8,136,128]{2,1,0:T(8,128)}), f32[8,136,128]{2,1,0:T(8,128)S(1)}, u32[]{:S(2)}, u32[]{:S(2)}) async-start(f32[8,136,128]{2,1,0:T(8,128)} %get-tuple-element.20), calls=%async_computation | async-start | bytes 1114112 | tf_op jit(solution)/shard_map/all_to_all | solution.py:614
  25.8 20.9 %collective-permute-start.5 = (f32[32,4224]{1,0:T(8,128)S(1)}, f32[32,4224]{1,0:T(8,128)S(1)}, u32[]{:S(2)}, u32[]{:S(2)}) collective-permute-start(f32[32,4224]{1,0:T(8,128)S(1)} %get-tuple-element.19.value_ref), channel_id=1, source_target_pairs={{0,32},{32,64},{64,96},{96,128},{128,160},{160,192},{192,224},{1,3... | collective-permute-start | bytes 1622024 | tf_op jit(solution)/shard_map/ppermute | solution.py:615
  43.0 15.6 %all-to-all-start.1 = ((f32[8,128,128]{2,1,0:T(8,128)}), f32[8,128,128]{2,1,0:T(8,128)S(1)}, u32[]{:S(2)}, u32[]{:S(2)}) async-start(f32[8,128,128]{2,1,0:T(8,128)} %coarse_solve.1), calls=%async_computation.1 | async-start | bytes 1048576 | tf_op jit(solution)/shard_map/all_to_all | solution.py:617

commit v5 on v4

--- a/solution.py
+++ b/solution.py
@@ -293,16 +293,13 @@
     weights_ref,
     out_ref,
     value_ref,
-    own_ref,
     even_ref,
     odd_ref,
-    sem,
 ):
     steps, _, length = forcing_ref.shape
     tiles = length // LANES
     guess_at, initial_at = left_ref.shape[0] - 2, left_ref.shape[0] - 1
-    own = pltpu.make_async_copy(guess_ref.at[0], own_ref, sem)
-    own.start()
+    own_ref = guess_ref.at[0]
     is_first = lax.axis_index("tm") == 0
 
     def begin(k):
@@ -335,7 +332,6 @@
     end = states[steps % 2]
     halo = join_halo(tile_of(end, tiles + 1), tile_of(end, 0))
     value_ref[:, length:] = halo
-    own.wait()
     guess_halo = make_halo(
         left_ref[guess_at], right_ref[guess_at], tile_of(own_ref, 0), tile_of(own_ref, tiles - 1)
     )
@@ -357,7 +353,6 @@
 ):
     steps, _, length = forcing.shape
     rows = length // groups // LANES * ROWS + RIM
-    anywhere = pl.BlockSpec(memory_space=pl.ANY)
     vmem = pl.BlockSpec(memory_space=pltpu.VMEM)
     return pl.pallas_call(
         first_kernel,
@@ -365,13 +360,11 @@
             pltpu.VMEM((groups, rows, LANES), jnp.float32),
             pltpu.VMEM((ROWS, length + LANES), jnp.float32),
         ),
-        in_specs=[vmem, vmem, vmem, vmem, anywhere, vmem, vmem, vmem, vmem, vmem],
+        in_specs=[vmem, vmem, vmem, vmem, vmem, vmem, vmem, vmem, vmem, vmem],
         out_specs=(vmem, vmem),
         scratch_shapes=[
-            pltpu.VMEM((ROWS, length), jnp.float32),
             pltpu.VMEM((ROWS, length + 2 * LANES), jnp.float32),
             pltpu.VMEM((ROWS, length + 2 * LANES), jnp.float32),
-            pltpu.SemaphoreType.DMA,
         ],
         compiler_params=pltpu.CompilerParams(vmem_limit_bytes=VMEM_LIMIT),
         cost_estimate=cost(steps, length, forcing.size),

time: 59.8 us -> 59.7 us (level)
  no operation moved by 1% of the time
where the time goes in v5:
time: 59.7 us; the launch traced here: 59.4 us
  waiting for transfers between devices  23.2 us (39%)
  Pallas kernels  18.5 us (31%)
  starting transfers between devices  17.6 us (29%)
    all_to_all x2, waiting for transfers between devices, body(): parts = lax.all_to_all(parts, 'tm', 0, 0, tiled=True)  15.8 us
    ppermute x1, waiting for transfers between devices, body(): left = lax.ppermute(high, 'space', up)  7.31 us
    all_to_all x2, starting transfers between devices, body(): parts = lax.all_to_all(parts, 'tm', 0, 0, tiled=True)  7.21 us
    pallas_call x1, Pallas kernels, second_chain(): pl.pallas_call(second_kernel, out_shape=jax.ShapeDtypeStruct(forcing.shap...  5.37 us
    pallas_call x1, Pallas kernels, coarse_solve(): pl.pallas_call(coarse_kernel, out_shape=pltpu.VMEM((groups, ROWS * tiles,...  4.05 us
    ppermute x1, starting transfers between devices, body(): begin = lax.ppermute(value, 'tm', to_next[:-1])  3.85 us
    pallas_call x1, Pallas kernels, first_chain(): pl.pallas_call(first_kernel, out_shape=(pltpu.VMEM((groups, rows, LANES),...  3.26 us
    pallas_call x1, Pallas kernels, prepare(): pl.pallas_call(prepare_kernel, out_shape=(pltpu.VMEM((OPERATORS, 4 * ROWS...  2.94 us
  transfers between devices with their start and end apart: 8, of which 3 were waited for; matrix products, arithmetic and copies ran while one was open for 0% of the time, Pallas kernels for 24%

profile of v5, /device:TPU:104, one launch (start us, length us, event | category | flops | bytes accessed | tf_op | source)
XLA Modules:
  0.0 59.4 jit_solution(8845092637588453655)
XLA Ops:
  0.0 0.0 copy-start.2
  0.0 0.0 copy-start.3
  0.0 1.5 %collective-permute-start.2 = (f32[32,4096]{1,0:T(8,128)}, f32[32,4096]{1,0:T(8,128)S(1)}, u32[]{:S(2)}, u32[]{:S(2)}) collective-permute-start(f32[32,4096]{1,0:T(8,128)} %bitcast.1), channel_id=1, source_target_pairs={{0,32},{32,64},{64,96},{96,128},{128,160},{160,192},{192,224},{224... | collective-permute-start | bytes 1572872 | tf_op jit(solution)/shard_map/ppermute | solution.py:586
  1.5 1.8 %edges.1 = (f32[10,8,128]{2,1,0:T(8,128)}, f32[10,8,128]{2,1,0:T(8,128)}, f32[8,128]{1,0:T(8,128)}, f32[8,128]{1,0:T(8,128)}) custom-call(f32[8,32,4096]{2,1,0:T(8,128)} %forcing_ref.3, f32[8,32,4096]{2,1,0:T(8,128)} %forcing_ref.3, f32[1,32,4096]{2,1,0:T(8,128)} %guess_ref.1, f32[1,32,4096]{2,1,0:T(8,128)} %guess_ref.1, f32[32,4096]{1,0:T(8,128)} %initial_ref.3, ...), custom_call_target="tpu_custom_call" | custom-call | tf_op jit(solution)/shard_map/edges/pallas_call | solution.py:233
  3.2 0.0 collective-permute-start
  3.3 1.7 %collective-permute-start.1 = (f32[10,8,128]{2,1,0:T(8,128)}, f32[10,8,128]{2,1,0:T(8,128)S(1)}, u32[]{:S(2)}, u32[]{:S(2)}) collective-permute-start(f32[10,8,128]{2,1,0:T(8,128)} %get-tuple-element.15), channel_id=1, source_target_pairs={{1,0},{2,1},{3,2},{4,3},{5,4},{6,5},{7,6},{8,7},{9,8},{10,9},{11,1... | collective-permute-start | bytes 122888 | tf_op jit(solution)/shard_map/ppermute | solution.py:588
  5.0 2.5 %collective-permute-start.3 = (f32[8,128]{1,0:T(8,128)}, f32[8,128]{1,0:T(8,128)S(1)}, u32[]{:S(2)}, u32[]{:S(2)}) collective-permute-start(f32[8,128]{1,0:T(8,128)} %get-tuple-element.16), channel_id=1, source_target_pairs={{0,33},{1,34},{2,35},{3,36},{4,37},{5,38},{6,39},{7,40},{8,41},{9,... | collective-permute-start | bytes 12296 | tf_op jit(solution)/shard_map/ppermute | solution.py:591
  7.5 0.0 copy-start
  7.5 0.0 copy-start.1
  7.5 0.8 %collective-permute-start.4 = (f32[8,128]{1,0:T(8,128)}, f32[8,128]{1,0:T(8,128)S(1)}, u32[]{:S(2)}, u32[]{:S(2)}) collective-permute-start(f32[8,128]{1,0:T(8,128)} %get-tuple-element.17), channel_id=1, source_target_pairs={{1,32},{2,33},{3,34},{4,35},{5,36},{6,37},{7,38},{8,39},{9,40},{10... | collective-permute-start | bytes 12296 | tf_op jit(solution)/shard_map/ppermute | solution.py:590
  8.3 0.0 copy-done.2
  8.3 0.0 copy-done.3
  8.3 2.9 %prepare.1 = (bf16[304,128]{1,0:T(8,128)(2,1)S(1)}, f32[8,32,4096]{2,1,0:T(8,128)S(1)}) custom-call(f32[4,16,16]{2,1,0:T(8,128)S(1)} %copy-done.2, f32[4,16,16]{2,1,0:T(8,128)S(1)} %copy-done.3, f32[8,32,4096]{2,1,0:T(8,128)} %forcing_ref.3), custom_call_target="tpu_custom_call" | custom-call | tf_op jit(solution)/shard_map/prepare/pallas_call | solution.py:193
  11.3 7.3 %collective-permute-done.left_ref = f32[10,8,128]{2,1,0:T(8,128)S(1)} collective-permute-done((f32[10,8,128]{2,1,0:T(8,128)}, f32[10,8,128]{2,1,0:T(8,128)S(1)}, u32[]{:S(2)}, u32[]{:S(2)}) %collective-permute-start) | collective-permute-done | bytes 40992 | tf_op jit(solution)/shard_map/ppermute | solution.py:589
  18.6 0.0 collective-permute-done.1.right_ref
  18.6 0.2 source_halos.1.source_halo_ref
  18.8 0.0 collective-permute-done.3.begin_left_ref
  18.8 0.0 collective-permute-done.4.begin_right_ref
  18.9 0.0 collective-permute-done.2.begin_ref
  18.9 0.0 copy-done
  18.9 0.0 copy-done.1
  18.9 3.3 %first_chain.1 = (f32[8,136,128]{2,1,0:T(8,128)}, f32[32,4224]{1,0:T(8,128)S(1)}) custom-call(f32[8,32,4096]{2,1,0:T(8,128)S(1)} %get-tuple-element.13.forcing_ref, f32[8,32,128]{2,1,0:T(8,128)S(1)} %source_halos.1.source_halo_ref, f32[32,4096]{1,0:T(8,128)S(1)} %collective-permute-done.2.begin_ref, f32[32,4096]{1,0:T(8,128)S(1)} %copy-done.1, ...), custom_call_target="tpu_custom_call" | custom-call | flops 5368709120 | bytes 8388608 | tf_op jit(solution)/shard_map/first_chain/pallas_call | solution.py:357
  22.1 3.5 %all-to-all-start = ((f32[8,136,128]{2,1,0:T(8,128)}), f32[8,136,128]{2,1,0:T(8,128)S(1)}, u32[]{:S(2)}, u32[]{:S(2)}) async-start(f32[8,136,128]{2,1,0:T(8,128)} %get-tuple-element.20), calls=%async_computation | async-start | bytes 1114112 | tf_op jit(solution)/shard_map/all_to_all | solution.py:607
  25.7 3.8 %collective-permute-start.5 = (f32[32,4224]{1,0:T(8,128)S(1)}, f32[32,4224]{1,0:T(8,128)S(1)}, u32[]{:S(2)}, u32[]{:S(2)}) collective-permute-start(f32[32,4224]{1,0:T(8,128)S(1)} %get-tuple-element.19.value_ref), channel_id=1, source_target_pairs={{0,32},{32,64},{64,96},{96,128},{128,160},{160,192},{192,224},{1,3... | collective-permute-start | bytes 1622024 | tf_op jit(solution)/shard_map/ppermute | solution.py:608
  29.5 9.3 %all-to-all-done.parts_ref = f32[8,136,128]{2,1,0:T(8,128)S(1)} async-done(((f32[8,136,128]{2,1,0:T(8,128)}), f32[8,136,128]{2,1,0:T(8,128)S(1)}, u32[]{:S(2)}, u32[]{:S(2)}) %all-to-all-start) | async-done | bytes 557088 | tf_op jit(solution)/shard_map/all_to_all | solution.py:607
  38.9 4.0 %coarse_solve.1 = f32[8,128,128]{2,1,0:T(8,128)} custom-call(f32[8,136,128]{2,1,0:T(8,128)S(1)} %all-to-all-done.parts_ref, bf16[304,128]{1,0:T(8,128)(2,1)S(1)} %get-tuple-element.18.weights_ref), custom_call_target="tpu_custom_call" | custom-call | flops 8053063680 | bytes 1114112 | tf_op jit(solution)/shard_map/coarse_solve/pallas_call | solution.py:439
  42.9 3.7 %all-to-all-start.1 = ((f32[8,128,128]{2,1,0:T(8,128)}), f32[8,128,128]{2,1,0:T(8,128)S(1)}, u32[]{:S(2)}, u32[]{:S(2)}) async-start(f32[8,128,128]{2,1,0:T(8,128)} %coarse_solve.1), calls=%async_computation.1 | async-start | bytes 1048576 | tf_op jit(solution)/shard_map/all_to_all | solution.py:610
  46.6 0.0 collective-permute-done.5.begin_ref
  46.6 5.4 %second_chain.1.states_ref = f32[8,32,4096]{2,1,0:T(8,128)} custom-call(f32[8,32,4096]{2,1,0:T(8,128)} %forcing_ref.3, f32[8,32,128]{2,1,0:T(8,128)S(1)} %source_halos.1.source_halo_ref, f32[32,4224]{1,0:T(8,128)S(1)} %collective-permute-done.5.begin_ref, f32[32,4096]{1,0:T(8,128)S(1)} %copy-done.1, f32[10,8,128]{2,1,0:T(8,128)S(1)} %collective-permute-done.left_ref, ...), custom_call_target="tpu_custom_call" | custom-call | flops 5368709120 | bytes 16777216 | tf_op jit(solution)/shard_map/second_chain/pallas_call | solution.py:519
  52.0 6.5 %all-to-all-done.1.parts_ref = f32[8,128,128]{2,1,0:T(8,128)S(1)} async-done(((f32[8,128,128]{2,1,0:T(8,128)}), f32[8,128,128]{2,1,0:T(8,128)S(1)}, u32[]{:S(2)}, u32[]{:S(2)}) %all-to-all-start.1) | async-done | bytes 524320 | tf_op jit(solution)/shard_map/all_to_all | solution.py:610
  58.5 0.8 %correct_last.1 = f32[8,32,4096]{2,1,0:T(8,128)} custom-call(f32[32,4224]{1,0:T(8,128)S(1)} %get-tuple-element.19.value_ref, f32[8,128,128]{2,1,0:T(8,128)S(1)} %all-to-all-done.1.parts_ref, f32[8,32,4096]{2,1,0:T(8,128)} %second_chain.1.states_ref), custom_call_target="tpu_custom_call", output_to_operand_aliasing={{}: (2, {})} | custom-call | tf_op jit(solution)/shard_map/correct_last/pallas_call | solution.py:560
Async XLA Ops:
  0.0 8.3 %copy-start.2 = (f32[4,16,16]{2,1,0:T(8,128)S(1)}, f32[4,16,16]{2,1,0:T(8,128)}, u32[]{:S(2)}) copy-start(f32[4,16,16]{2,1,0:T(8,128)} %fine_ref.1) | copy-start | bytes 12292
  0.0 8.3 %copy-start.3 = (f32[4,16,16]{2,1,0:T(8,128)S(1)}, f32[4,16,16]{2,1,0:T(8,128)}, u32[]{:S(2)}) copy-start(f32[4,16,16]{2,1,0:T(8,128)} %coarse_ref.1) | copy-start | bytes 12292
  0.0 18.9 %collective-permute-start.2 = (f32[32,4096]{1,0:T(8,128)}, f32[32,4096]{1,0:T(8,128)S(1)}, u32[]{:S(2)}, u32[]{:S(2)}) collective-permute-start(f32[32,4096]{1,0:T(8,128)} %bitcast.1), channel_id=1, source_target_pairs={{0,32},{32,64},{64,96},{96,128},{128,160},{160,192},{192,224},{224... | collective-permute-start | bytes 1572872 | tf_op jit(solution)/shard_map/ppermute | solution.py:586
  3.2 15.3 %collective-permute-start = (f32[10,8,128]{2,1,0:T(8,128)}, f32[10,8,128]{2,1,0:T(8,128)S(1)}, u32[]{:S(2)}, u32[]{:S(2)}) collective-permute-start(f32[10,8,128]{2,1,0:T(8,128)} %get-tuple-element.14), channel_id=1, source_target_pairs={{0,1},{1,2},{2,3},{3,4},{4,5},{5,6},{6,7},{7,8},{8,9},{9,10},{10,1... | collective-permute-start | bytes 122888 | tf_op jit(solution)/shard_map/ppermute | solution.py:589
  3.3 15.3 %collective-permute-start.1 = (f32[10,8,128]{2,1,0:T(8,128)}, f32[10,8,128]{2,1,0:T(8,128)S(1)}, u32[]{:S(2)}, u32[]{:S(2)}) collective-permute-start(f32[10,8,128]{2,1,0:T(8,128)} %get-tuple-element.15), channel_id=1, source_target_pairs={{1,0},{2,1},{3,2},{4,3},{5,4},{6,5},{7,6},{8,7},{9,8},{10,9},{11,1... | collective-permute-start | bytes 122888 | tf_op jit(solution)/shard_map/ppermute | solution.py:588
  5.0 13.8 %collective-permute-start.3 = (f32[8,128]{1,0:T(8,128)}, f32[8,128]{1,0:T(8,128)S(1)}, u32[]{:S(2)}, u32[]{:S(2)}) collective-permute-start(f32[8,128]{1,0:T(8,128)} %get-tuple-element.16), channel_id=1, source_target_pairs={{0,33},{1,34},{2,35},{3,36},{4,37},{5,38},{6,39},{7,40},{8,41},{9,... | collective-permute-start | bytes 12296 | tf_op jit(solution)/shard_map/ppermute | solution.py:591
  7.5 11.4 %copy-start = (f32[1,32,4096]{2,1,0:T(8,128)S(1)}, f32[1,32,4096]{2,1,0:T(8,128)}, u32[]{:S(2)}) copy-start(f32[1,32,4096]{2,1,0:T(8,128)} %guess_ref.1) | copy-start | bytes 1572868
  7.5 11.4 %copy-start.1 = (f32[32,4096]{1,0:T(8,128)S(1)}, f32[32,4096]{1,0:T(8,128)}, u32[]{:S(2)}) copy-start(f32[32,4096]{1,0:T(8,128)} %initial_ref.3) | copy-start | bytes 1572868
  7.5 11.4 %collective-permute-start.4 = (f32[8,128]{1,0:T(8,128)}, f32[8,128]{1,0:T(8,128)S(1)}, u32[]{:S(2)}, u32[]{:S(2)}) collective-permute-start(f32[8,128]{1,0:T(8,128)} %get-tuple-element.17), channel_id=1, source_target_pairs={{1,32},{2,33},{3,34},{4,35},{5,36},{6,37},{7,38},{8,39},{9,40},{10... | collective-permute-start | bytes 12296 | tf_op jit(solution)/shard_map/ppermute | solution.py:590
  22.1 16.7 %all-to-all-start = ((f32[8,136,128]{2,1,0:T(8,128)}), f32[8,136,128]{2,1,0:T(8,128)S(1)}, u32[]{:S(2)}, u32[]{:S(2)}) async-start(f32[8,136,128]{2,1,0:T(8,128)} %get-tuple-element.20), calls=%async_computation | async-start | bytes 1114112 | tf_op jit(solution)/shard_map/all_to_all | solution.py:607
  25.7 20.9 %collective-permute-start.5 = (f32[32,4224]{1,0:T(8,128)S(1)}, f32[32,4224]{1,0:T(8,128)S(1)}, u32[]{:S(2)}, u32[]{:S(2)}) collective-permute-start(f32[32,4224]{1,0:T(8,128)S(1)} %get-tuple-element.19.value_ref), channel_id=1, source_target_pairs={{0,32},{32,64},{64,96},{96,128},{128,160},{160,192},{192,224},{1,3... | collective-permute-start | bytes 1622024 | tf_op jit(solution)/shard_map/ppermute | solution.py:608
  42.9 15.6 %all-to-all-start.1 = ((f32[8,128,128]{2,1,0:T(8,128)}), f32[8,128,128]{2,1,0:T(8,128)S(1)}, u32[]{:S(2)}, u32[]{:S(2)}) async-start(f32[8,128,128]{2,1,0:T(8,128)} %coarse_solve.1), calls=%async_computation.1 | async-start | bytes 1048576 | tf_op jit(solution)/shard_map/all_to_all | solution.py:610
